TPU v7x, 32 devices: a whole 2x2x4 slice. The times are simulated.
32 devices in a mesh: groups: 2 (over x), mp: 16 (over z, y, core).
Axes of the slice: x: 2, y: 2, z: 4, core: 2. Of those that a mesh axis runs over, the one named last changes fastest.
Arguments:
- features: bfloat16 [32, 256, 128, 128], P(None, ('groups', 'mp')), parts along dimension 1, may hold values from -6 to 6
- cotangent: bfloat16 [32, 256, 128, 128], P(None, ('groups', 'mp')), parts along dimension 1, may hold values from -9 to 9
- spectral_weight: float32 [256, 2, 16, 32, 32], P('mp'), may hold values from -9 to 9
- pointwise_weight: bfloat16 [32, 32], replicated, may hold values from -1 to 1
- biases: float32 [32], replicated, may hold values from -3 to 3
Outputs:
- features_grad: bfloat16 [32, 256, 128, 128], P(None, ('groups', 'mp')), parts along dimension 1
- spectral_grad: float32 [512, 2, 16, 32, 32], P(('groups', 'mp')), parts along dimension 0
- pointwise_grad: float32 [64, 32], P('groups'), parts along dimension 0
- biases_grad: float32 [64], P('groups'), parts along dimension 0
There are 2 independent parts, one for each index of `groups`. A program takes and returns all parts, laid end to end along the dimension named above; an argument that names none is the same for every part. Nothing has to cross between parts.
All inputs are finite; a program needn't handle non-finite values.
Results may differ from a plain program's by a relative error of at most 0.007.
Values sent between devices are 32-bit elements; how exact they have to be, the bound alone decides.
A program may use at most 128 MiB of HBM per device.

v0:
```python
import functools
import math

import jax
import jax.numpy as jnp
import ml_dtypes
import numpy as np
from jax import lax
from jax.experimental import pallas as pl
from jax.experimental.pallas import tpu as pltpu
from jax.sharding import PartitionSpec as P

C = 32
NX = 128
NY = 128
NZ = 128
KX = 16
KY = 16
KZ = 16
SCALE = 1.0 / (NX * NY * NZ)
OCT = 8
GROUPS = C // OCT
GLANES = 2 * OCT * KZ
LANES = 128
SAVES = 4
BF = jnp.bfloat16
F32 = jnp.float32
precise = lax.Precision.HIGHEST
VMEM = pl.BlockSpec(memory_space=pltpu.VMEM)
HBM = pl.BlockSpec(memory_space=pl.ANY)


def trig(length, mode_count, signed):
    freqs = np.arange(mode_count) - (mode_count // 2 if signed else 0)
    spots = np.arange(length)
    phases = (spots[:, None] * freqs[None, :] % length) * (2.0 * math.pi / length)
    return np.cos(phases), np.sin(phases)


def low(table):
    return np.asarray(table, np.float32).astype(ml_dtypes.bfloat16)


def tables(rows):
    zc, zs = trig(NZ, KZ, False)
    yc, ys = trig(NY, KY, True)
    xc, xs = trig(NX, KX, True)
    wz = np.where(np.arange(KZ) == 0, 1.0, 2.0) * SCALE
    eye = np.eye(rows)
    fy = np.einsum("syj,xw->sjxwy", np.stack([yc, ys]), eye).reshape(2 * KY * rows, rows * NY)
    gy = np.einsum("syj,xw->xysjw", np.stack([yc, -ys]), eye).reshape(rows * NY, 2 * KY * rows)
    zc_low = low(zc).astype(np.float64)
    zs_low = low(zs).astype(np.float64)
    oct_eye = np.eye(OCT)
    block = np.stack([np.stack([zc_low, -zs_low]), np.stack([-zs_low, -zc_low])])
    fz = np.einsum("srzk,ab->aszrbk", block, oct_eye).reshape(OCT * 2 * NZ, 2 * OCT * KZ)
    fz_w = (fz.reshape(-1, KZ) * wz).reshape(fz.shape)
    back = np.stack([np.stack([zc, zs]), np.stack([-zs, zc])])
    gz = np.einsum("rqzk,ab->rakbqz", back, oct_eye).reshape(2 * OCT * KZ, OCT * 2 * NZ)
    gz_w = (np.einsum("rqzk,ab,k->rakbqz", back, oct_eye, wz)).reshape(gz.shape)
    fx = np.concatenate([xc.T, xs.T], 0).astype(np.float32)
    gx = np.concatenate([xc, xs], 0).astype(np.float32)
    fx2 = np.block([[xc.T, xs.T], [-xs.T, xc.T]]).astype(np.float32)
    gx2 = np.block([[xc, -xs], [xs, xc]]).astype(np.float32)
    return low(fy), low(gy), low(fz), low(fz_w), low(gz), low(gz_w), fx, gx, fx2, gx2


def dot(a, b):
    return jnp.dot(a, b, preferred_element_type=F32)


def forward_group(src, g, fy, fz, lines):
    parts = []
    for q in range(0, OCT, 2):
        pair = jnp.concatenate([src[g * OCT + q], src[g * OCT + q + 1]], axis=1)
        both = dot(fy[...], pair).astype(BF)
        for h in range(2):
            piece = both[:, h * NZ : (h + 1) * NZ]
            parts += [piece[:lines], piece[lines:]]
    return dot(jnp.concatenate(parts, axis=1), fz[...])


def plane_back(src, gz, gy, out):
    @pl.loop(0, GROUPS)
    def _(g):
        lhs = src[:, pl.ds(pl.multiple_of(g * GLANES, GLANES), GLANES)].astype(BF)
        u = dot(lhs, gz[...]).astype(BF)
        for q in range(0, OCT, 2):
            cols = []
            for h in range(2):
                o = q + h
                cols.append(
                    jnp.concatenate(
                        [u[:, (2 * o + r) * NZ : (2 * o + r + 1) * NZ] for r in range(2)], axis=0
                    )
                )
            res = dot(gy[...], jnp.concatenate(cols, axis=1))
            out[g * OCT + q] = res[:, :NZ]
            out[g * OCT + q + 1] = res[:, NZ:]


def plain_forward(src, fy, fz, out, lines):
    @pl.loop(0, GROUPS)
    def _(g):
        at = pl.multiple_of(g * GLANES, GLANES)
        out[:, pl.ds(at, GLANES)] = forward_group(src, g, fy, fz, lines)


def load_groups(hbm, buf, sems):
    copies = []
    for g in range(GROUPS):
        part = pl.ds(g * OCT, OCT)
        copies.append(pltpu.make_async_copy(hbm.at[part], buf.at[part], sems.at[g]))
        copies[-1].start()
    return copies


def greet(n):
    me = lax.axis_index("mp")

    @pl.loop(1, n)
    def _(s):
        pl.semaphore_signal(
            pltpu.get_barrier_semaphore(),
            inc=1,
            device_id={"mp": lax.rem(me + s, n)},
            device_id_type=pl.DeviceIdType.MESH,
        )


def remote(src, dst, send, recv, peer):
    return pltpu.make_async_remote_copy(
        src_ref=src,
        dst_ref=dst,
        send_sem=send,
        recv_sem=recv,
        device_id={"mp": peer},
        device_id_type=pl.DeviceIdType.MESH,
    )


def send_half(n, half, src, dst, send, recv, own):
    me = lax.axis_index("mp")
    wide = GLANES * GROUPS // 2
    lanes = pl.ds(half * wide, wide)

    @pl.loop(1, n)
    def _(s):
        peer = lax.rem(me + s, n)
        remote(
            src.at[peer, :, lanes],
            dst.at[me, :, lanes],
            send.at[half, peer],
            recv.at[half, me],
            peer,
        ).start()

    mine = pltpu.make_async_copy(src.at[me, :, lanes], dst.at[me, :, lanes], own.at[half])
    mine.start()
    return mine


def wait_half(n, half, src, dst, send, recv):
    me = lax.axis_index("mp")
    wide = GLANES * GROUPS // 2
    lanes = pl.ds(half * wide, wide)

    @pl.loop(1, n)
    def _(s):
        peer = lax.rem(me + s, n)
        both = remote(
            src.at[peer, :, lanes],
            dst.at[peer, :, lanes],
            send.at[half, peer],
            recv.at[half, peer],
            peer,
        )
        both.wait_recv()
        both.wait_send()


def spread_out(rows, n, field, fy, fz, fx2, spec, src, dst, send, recv, own, ready):
    mine = []
    for half in range(2):
        for g in range(half * GROUPS // 2, (half + 1) * GROUPS // 2):
            ready(g)
            res = forward_group(field, g, fy, fz, KY * rows)
            src[:, :, g * GLANES : (g + 1) * GLANES] = res.reshape(KY, rows, GLANES)
        if half == 0:
            pl.semaphore_wait(pltpu.get_barrier_semaphore(), n - 1)
        mine.append(send_half(n, half, src, dst, send, recv, own))
    each = GLANES // 2
    for half in range(2):
        mine[half].wait()
        wait_half(n, half, src, dst, send, recv)
        for g in range(half * GROUPS // 2, (half + 1) * GROUPS // 2):
            pair = [
                dst[:, :, g * GLANES + r * each : g * GLANES + (r + 1) * each].reshape(NX, each)
                for r in range(2)
            ]
            spec[:, g * each : (g + 1) * each] = jnp.dot(
                fx2[...],
                jnp.concatenate(pair, axis=0),
                precision=precise,
                preferred_element_type=F32,
            )


def analysis_kernel(rows, n, feat_hbm, fy, fz, fx2, spec, feat, load, src, dst, send, recv, own):
    greet(n)
    loads = load_groups(feat_hbm, feat, load)
    spread_out(
        rows, n, feat, fy, fz, fx2, spec, src, dst, send, recv, own, lambda g: loads[g].wait()
    )


def forward_kernel(rows, feat, fy, fz, out):
    plain_forward(feat, fy, fz, out, KY * rows)


TILE = 16
STEP = 4


def tile_of(ref, t):
    at = pl.multiple_of(t * TILE, TILE)
    return ref[:, pl.ds(at, TILE), :].reshape(C * TILE, NZ)


def put_tile(ref, t, value):
    at = pl.multiple_of(t * TILE, TILE)
    ref[:, pl.ds(at, TILE), :] = value.reshape(C, TILE, NZ)


def widen(weight):
    n = C * TILE
    row = lax.broadcasted_iota(jnp.int32, (n, C), 0) // TILE
    up = jnp.where(row == lax.broadcasted_iota(jnp.int32, (n, C), 1), 1.0, 0.0).astype(BF)
    left = dot(up, weight).astype(BF)
    full = lax.dot_general(left, up, (((1,), (1,)), ((), ())), preferred_element_type=F32)
    ri = lax.broadcasted_iota(jnp.int32, (n, n), 0)
    ci = lax.broadcasted_iota(jnp.int32, (n, n), 1)
    return jnp.where(ri % TILE == ci % TILE, full, 0.0).astype(BF)


def middle_kernel(
    rows, n, feat_hbm, cot_hbm, modes, weight, bias, gz, gy, fy, fz, fx2, pg_hbm, part, sums,
    field, acc, bacc, kron, feat, cot, pg, fsem, csem, psem, *net,
):
    if net:
        greet(n)
    loads = load_groups(feat_hbm, feat, fsem) + load_groups(cot_hbm, cot, csem)
    kron[...] = widen(weight[...])
    acc[...] = jnp.zeros_like(acc)
    bacc[...] = jnp.zeros_like(bacc)
    plane_back(modes, gz, gy, field)
    for copy in loads:
        copy.wait()

    @pl.loop(0, rows * NY // (STEP * TILE))
    def _(s):
        f = jnp.concatenate([tile_of(feat, STEP * s + h) for h in range(STEP)], axis=1)
        mix = dot(kron[...], f)
        gs = []
        for h in range(STEP):
            t = STEP * s + h
            x = mix[:, h * NZ : (h + 1) * NZ] + tile_of(field, t) + bias[...]
            x2 = x * x
            a = math.sqrt(2.0 / math.pi)
            th = jnp.tanh(x * (a + (a * 0.044715) * x2))
            d = (0.5 + 0.5 * th) * (1.0 + (x * (1.0 - th)) * (a + (3.0 * a * 0.044715) * x2))
            g = (tile_of(cot, t).astype(F32) * d).astype(BF)
            put_tile(pg, t, g)
            gs.append(g)
        bacc[...] += sum(g.astype(F32) for g in gs)
        g = jnp.concatenate(gs, axis=1)
        acc[...] += lax.dot_general(g, f, (((1,), (1,)), ((), ())), preferred_element_type=F32)

    save = pltpu.make_async_copy(pg, pg_hbm, psem)
    save.start()
    size = C * TILE
    ri = lax.broadcasted_iota(jnp.int32, (size, size), 0)
    ci = lax.broadcasted_iota(jnp.int32, (size, size), 1)
    masked = jnp.where(ri % TILE == ci % TILE, acc[...], 0.0)
    rows_sum = jnp.sum(masked.reshape(C, TILE, size), axis=1)
    fold = jnp.where(
        lax.broadcasted_iota(jnp.int32, (size, LANES), 0) // TILE
        == lax.broadcasted_iota(jnp.int32, (size, LANES), 1),
        1.0,
        0.0,
    ).astype(F32)
    pw = jnp.dot(rows_sum, fold, precision=precise, preferred_element_type=F32)
    by_row = jnp.sum(bacc[...].reshape(C, TILE, NZ), axis=1)
    lane = lax.broadcasted_iota(jnp.int32, (C, LANES), 1)
    sums[...] = pw + jnp.where(lane == C, jnp.sum(by_row, axis=1, keepdims=True), 0.0)
    if net:
        spread_out(rows, n, pg, fy, fz, fx2, part, *net, lambda g: None)
    else:
        plain_forward(pg, fy, fz, part, KY * rows)
    save.wait()


def last_kernel(rows, pg_hbm, modes, weight, gz, gy, out_hbm, field, kron, pg, out, fsem, osem):
    loads = load_groups(pg_hbm, pg, fsem)
    kron[...] = widen(weight[...])
    plane_back(modes, gz, gy, field)
    for copy in loads:
        copy.wait()
    saves = []
    cells = rows * NY // SAVES
    for piece in range(SAVES):

        @pl.loop(0, cells // (STEP * TILE))
        def _(i):
            s = piece * (cells // (STEP * TILE)) + i
            f = jnp.concatenate([tile_of(pg, STEP * s + h) for h in range(STEP)], axis=1)
            mix = dot(kron[...], f)
            for h in range(STEP):
                t = STEP * s + h
                r = mix[:, h * NZ : (h + 1) * NZ] + tile_of(field, t)
                put_tile(out, t, r.astype(BF))

        at = pl.ds(piece * cells, cells)
        saves.append(pltpu.make_async_copy(out.at[:, at], out_hbm.at[:, at], osem.at[piece]))
        saves[-1].start()
    for copy in saves:
        copy.wait()


def exchange_kernel(n, arrays, spread, *refs):
    me = lax.axis_index("mp")
    greet(n)
    srcs = refs[:arrays]
    if spread:
        table, refs, lines = refs[arrays], refs[:arrays] + refs[arrays + 1 : -1], refs[-1]
        each = GLANES // 2
        for g in range(GROUPS):
            part = srcs[0][:, g * each : (g + 1) * each]
            both = jnp.dot(table[...], part, precision=precise, preferred_element_type=F32)
            for r in range(2):
                at = g * GLANES + r * each
                lines[:, :, at : at + each] = both[r * NX : (r + 1) * NX].reshape(n, NX // n, each)
        srcs = (lines, *srcs[1:])
    dsts = refs[arrays : 2 * arrays]
    send, recv, own = refs[2 * arrays :]
    pl.semaphore_wait(pltpu.get_barrier_semaphore(), n - 1)

    @pl.loop(1, n)
    def _(s):
        peer = lax.rem(me + s, n)
        for i in range(arrays):
            remote(
                srcs[i].at[peer], dsts[i].at[me], send.at[i, peer], recv.at[i, me], peer
            ).start()

    for i in range(arrays):
        mine = pltpu.make_async_copy(srcs[i].at[me], dsts[i].at[me], own.at[i])
        mine.start()
        mine.wait()

    @pl.loop(1, n)
    def _(s):
        peer = lax.rem(me + s, n)
        for i in range(arrays):
            both = remote(
                srcs[i].at[peer], dsts[i].at[peer], send.at[i, peer], recv.at[i, peer], peer
            )
            both.wait_recv()
            both.wait_send()


def exchange(xs, n, cid, table=None):
    shapes = [jax.ShapeDtypeStruct(x.shape, x.dtype) for x in xs]
    extra = []
    if table is not None:
        shapes[0] = jax.ShapeDtypeStruct((n, NX // n, 2 * C * KZ), F32)
        extra = [table]
    return pl.pallas_call(
        functools.partial(exchange_kernel, n, len(xs), table is not None),
        out_shape=shapes,
        in_specs=[VMEM] * (len(xs) + len(extra)),
        out_specs=[VMEM] * len(xs),
        scratch_shapes=[
            pltpu.SemaphoreType.DMA((len(xs), n)),
            pltpu.SemaphoreType.DMA((len(xs), n)),
            pltpu.SemaphoreType.DMA((len(xs),)),
        ]
        + [pltpu.VMEM(shapes[0].shape, F32)] * len(extra),
        compiler_params=pltpu.CompilerParams(
            collective_id=cid, has_side_effects=True, vmem_limit_bytes=16 << 20
        ),
        name=f"exchange{cid}",
    )(*xs, *extra)


def call(kernel, rows, outs, scratch, args, name, far=(), far_out=(), cid=None):
    outs = list(outs)
    params = {} if cid is None else {"collective_id": cid, "has_side_effects": True}
    return pl.pallas_call(
        functools.partial(kernel, rows),
        out_shape=outs,
        in_specs=[HBM if i in far else VMEM for i in range(len(args))],
        out_specs=[HBM if i in far_out else VMEM for i in range(len(outs))],
        scratch_shapes=scratch,
        compiler_params=pltpu.CompilerParams(vmem_limit_bytes=60 << 20, **params),
        name=name,
    )(*args)


def owner_blocks(part, n, rows):
    subs = n // KY
    if subs > 1:
        v = part.reshape(KY, rows, 2 * C, subs, KZ // subs)
        part = jnp.transpose(v, (0, 3, 1, 2, 4))
    return part.reshape(n, rows, 2 * C * KZ // subs)


def plane_blocks(got, n, rows):
    subs = n // KY
    if subs > 1:
        v = got.reshape(KY, subs, rows, 2 * C, KZ // subs)
        got = jnp.transpose(v, (0, 2, 3, 1, 4))
    return got.reshape(KY * rows, 2 * C * KZ)


def lines_forward(g, fx):
    g = g.reshape(NX, -1)
    t = jnp.einsum("qx,xl->ql", fx, g, precision=precise).reshape(2, KX, GROUPS, 2, OCT, -1)
    real = t[0, :, :, 0] + t[1, :, :, 1]
    imag = t[0, :, :, 1] - t[1, :, :, 0]
    real, imag = (jnp.transpose(v.reshape(KX, C, -1), (2, 0, 1)) for v in (real, imag))
    return real, imag


def lines_back(real, imag, gx, n, rows):
    u = jnp.stack([real, imag]).reshape(2, real.shape[0], KX, GROUPS, OCT)
    u = jnp.transpose(u, (2, 3, 0, 4, 1)).reshape(KX, -1)
    b = jnp.einsum("qa,al->ql", gx, u, precision=precise).reshape(2, NX, GROUPS, 2, -1)
    lines = jnp.stack([b[0, :, :, 0] - b[1, :, :, 1], b[0, :, :, 1] + b[1, :, :, 0]], 2)
    return lines.reshape(n, rows, -1)


def split_modes(spec):
    v = jnp.transpose(spec.reshape(2, KX, C, KZ), (0, 3, 1, 2))
    return v[0], v[1]


def join_modes(real, imag):
    return jnp.transpose(jnp.stack([real, imag]), (0, 2, 3, 1)).reshape(2 * KX, C * KZ)


def shards(features, cotangent, spectral_weight, pointwise_weight, biases):
    n = lax.axis_size("mp")
    rows = NX // n
    fy, gy, fz, fz_w, gz, gz_w, fx, gx, fx2, gx2 = [jnp.asarray(t) for t in tables(rows)]
    cells = rows * NY
    feat = features.reshape(C, cells, NZ)
    cot = cotangent.reshape(C, cells, NZ)
    bias = jnp.repeat(biases, TILE)[:, None]
    spread = jax.ShapeDtypeStruct((KY * rows, 2 * C * KZ), F32)
    whole = jax.ShapeDtypeStruct((C, cells, NZ), BF)
    field = pltpu.VMEM((C, cells, NZ), F32)
    block = pltpu.VMEM((C, cells, NZ), BF)
    wide = C * TILE
    dma = pltpu.SemaphoreType.DMA
    sems = dma((GROUPS,))
    fused = n == KY
    lines = pltpu.VMEM((n, rows, 2 * C * KZ), F32)
    net = [lines, lines, dma((2, n)), dma((2, n)), dma((2,))] if fused else []
    if fused:
        spread = jax.ShapeDtypeStruct((2 * KX, C * KZ), F32)
        spec = call(
            lambda r, *refs: analysis_kernel(r, n, *refs),
            rows,
            [spread],
            [block, sems, *net],
            (feat, fy, fz, fx2),
            "analysis",
            far=(0,),
            cid=1,
        )[0]
        v_r, v_i = split_modes(spec)
    else:
        part = call(forward_kernel, rows, [spread], [], (feat, fy, fz), "analysis")[0]
        v_r, v_i = lines_forward(exchange([owner_blocks(part, n, rows)], n, 1)[0], fx)
    w_r, w_i = spectral_weight[:, 0], spectral_weight[:, 1]
    s_r, s_i = v_r[..., None], v_i[..., None]
    u_r = jnp.sum(s_r * w_r - s_i * w_i, axis=2)
    u_i = jnp.sum(s_r * w_i + s_i * w_r, axis=2)
    if fused:
        modes = exchange([join_modes(u_r, u_i)], n, 2, gx2)[0]
    else:
        modes = exchange([lines_back(u_r, u_i, gx, n, rows)], n, 2)[0]
    pg, dpart, sums = call(
        lambda r, *refs: middle_kernel(r, n, *refs),
        rows,
        [whole, spread, jax.ShapeDtypeStruct((C, LANES), F32)],
        [
            field,
            pltpu.VMEM((wide, wide), F32),
            pltpu.VMEM((wide, NZ), F32),
            pltpu.VMEM((wide, wide), BF),
            block,
            block,
            block,
            sems,
            sems,
            dma,
            *net,
        ],
        (feat, cot, plane_blocks(modes, n, rows), pointwise_weight, bias, gz_w, gy, fy, fz_w, fx2),
        "middle",
        far=(0, 1),
        far_out=(0,),
        cid=3 if fused else None,
    )
    if fused:
        d_r, d_i = split_modes(dpart)
    else:
        d_r, d_i = lines_forward(exchange([owner_blocks(dpart, n, rows)], n, 3)[0], fx)
    e_r, e_i = d_r[:, :, None, :], d_i[:, :, None, :]
    m_r = jnp.sum(e_r * w_r + e_i * w_i, axis=3)
    m_i = jnp.sum(e_i * w_r - e_r * w_i, axis=3)
    packed = jnp.concatenate(
        [sums[:, :C].reshape(-1, LANES), jnp.pad(sums[:, C], (0, LANES - C))[None]], axis=0
    )
    mine = jnp.broadcast_to(packed, (n, *packed.shape))
    if fused:
        back, every = exchange([join_modes(m_r, m_i), mine], n, 4, gx2)
    else:
        back, every = exchange([lines_back(m_r, m_i, gx, n, rows), mine], n, 4)
    total = jnp.sum(every, axis=0)
    first = jnp.stack([v_r, -v_i], axis=1)[..., None]
    second = jnp.stack([v_i, v_r], axis=1)[..., None]
    spectral_grad = first * e_r[:, None] + second * e_i[:, None]
    grad = call(
        last_kernel,
        rows,
        [whole],
        [field, pltpu.VMEM((wide, wide), BF), block, block, sems, pltpu.SemaphoreType.DMA((SAVES,))],
        (pg, plane_blocks(back, n, rows), pointwise_weight.T, gz, gy),
        "synthesis",
        far=(0,),
        far_out=(0,),
    )[0]
    factor = float(NX * NY * NZ) ** (-0.5)
    total = total * factor
    return (grad.reshape(features.shape), spectral_grad, total[:-1].reshape(C, C), total[-1, :C])


def solution(mesh):
    return jax.shard_map(
        shards,
        mesh=mesh,
        in_specs=(
            P(None, ("groups", "mp"), None, None),
            P(None, ("groups", "mp"), None, None),
            P("mp", None, None, None, None),
            P(),
            P(),
        ),
        out_specs=(
            P(None, ("groups", "mp"), None, None),
            P(("groups", "mp"), None, None, None, None),
            P("groups", None),
            P("groups"),
        ),
        check_vma=False,
    )
```

profile of v0, /device:TPU:0, one launch (start us, length us, event | category | flops | bytes accessed | tf_op | source)
XLA Modules:
  0.0 141.8 jit_solution(4861514959181300141)
XLA Ops:
  0.6 1.4 copy.46
  2.0 0.7 broadcast_in_dim.11
  2.7 21.8 %analysis.1 = f32[32,512]{1,0:T(8,128)} custom-call(bf16[32,1024,128]{2,1,0:T(8,128)(2,1)} %bitcast.77, bf16[256,1024]{1,0:T(8,128)(2,1)} %constant.22.clone.refs_1_.refs_7_, bf16[2048,256]{1,0:T(8,128)(2,1)} %constant.24.clone.refs_2_, f32[32,256]{1,0:T(8,128)} %constant.28.clone.refs_3_.refs_9_), custom_call_target="tpu_custom_call" | custom-call | tf_op jit(solution)/shard_map/analysis/pallas_call | solution.py:399
  24.5 0.9 broadcast_in_dim_reshape.4.refs_4_
  25.4 1.0 reshape.61
  26.5 0.1 slice_bitcast_fusion.2
  26.6 0.1 copy.40
  26.7 0.1 copy.38
  26.9 5.5 %fusion.1 = (f32[16,16,32]{2,1,0:T(8,128)S(1)}, f32[16,16,32]{2,1,0:T(8,128)S(1)}) fusion(f32[16,2,16,32,32]{4,3,2,1,0:T(8,128)} %param.15, f32[16,16,32]{2,1,0:T(8,128)S(1)} %copy.40, f32[16,16,32]{2,1,0:T(8,128)S(1)} %copy.38), kind=kLoop, calls=%fused_computation.6 | loop fusion | flops 2080768 | bytes 2228224 | tf_op jit(solution)/shard_map/reduce_sum | solution.py:488
  32.4 0.0 copy-start.2
  32.4 0.2 copy.41
  32.7 0.3 reshape.62.refs_0_
  32.9 0.1 pad_maximum_fusion
  33.1 0.3 copy.47
  33.3 0.3 copy.49
  33.6 0.0 copy-done.2
  33.6 12.4 %exchange2.1 = f32[16,8,1024]{2,1,0:T(8,128)S(1)} custom-call(f32[32,512]{1,0:T(8,128)S(1)} %reshape.62.refs_0_, f32[256,32]{1,0:T(8,128)S(1)} %copy-done.2), custom_call_target="tpu_custom_call" | custom-call | tf_op jit(solution)/shard_map/exchange2/pallas_call | solution.py:378
  46.0 0.0 copy-start
  46.0 0.8 copy-done
  46.8 46.2 %middle.1 = (bf16[32,1024,128]{2,1,0:T(8,128)(2,1)}, f32[32,512]{1,0:T(8,128)}, f32[32,128]{1,0:T(8,128)}) custom-call(bf16[32,1024,128]{2,1,0:T(8,128)(2,1)} %bitcast.78, bf16[32,1024,128]{2,1,0:T(8,128)(2,1)} %bitcast.79, f32[128,1024]{1,0:T(8,128)} %bitcast.75, bf16[32,32]{1,0:T(8,128)(2,1)} %refs_3_.2, f32[512,1]{1,0:T(8,128)} %broadcast_in_dim_reshape.4.refs_4_, ...), custom_call_target="tpu_custom_call" | custom-call | tf_op jit(solution)/shard_map/middle/pallas_call | solution.py:399
  93.1 0.9 slice_reduce_fusion
  94.0 0.8 reshape.66
  94.8 1.0 reshape.64
  95.9 0.1 copy.43
  96.0 0.1 copy.44
  96.1 4.7 %fusion.5 = (f32[16,16,32]{2,1,0:T(8,128)S(1)}, f32[16,16,32]{2,1,0:T(8,128)S(1)}) fusion(f32[16,2,16,32,32]{4,3,2,1,0:T(8,128)} %param.15, f32[16,16,32]{2,1,0:T(8,128)S(1)} %copy.44, f32[16,16,32]{2,1,0:T(8,128)S(1)} %copy.43), kind=kLoop, calls=%fused_computation.10 | loop fusion | flops 2080768 | bytes 2228224 | tf_op jit(solution)/shard_map/reduce_sum | solution.py:522
  100.8 0.2 copy.45
  101.1 0.3 reshape.65.refs_0_
  101.3 16.5 %exchange4.1 = (f32[16,8,1024]{2,1,0:T(8,128)S(1)}, f32[16,9,128]{2,1,0:T(8,128)S(1)}) custom-call(f32[32,512]{1,0:T(8,128)S(1)} %reshape.65.refs_0_, f32[16,9,128]{2,1,0:T(8,128)S(1)} %broadcast_in_dim.13.refs_1_, f32[256,32]{1,0:T(8,128)S(1)} %copy-done.2), custom_call_target="tpu_custom_call" | custom-call | tf_op jit(solution)/shard_map/exchange4/pallas_call | solution.py:378
  117.8 0.0 copy-start.1
  117.8 0.8 copy-done.1
  118.6 15.0 %synthesis.1 = bf16[32,1024,128]{2,1,0:T(8,128)(2,1)} custom-call(bf16[32,1024,128]{2,1,0:T(8,128)(2,1)} %get-tuple-element.9.pg_hbm, f32[128,1024]{1,0:T(8,128)} %bitcast.76, bf16[32,32]{1,0:T(8,128)(2,1)} %bitcast.89, bf16[256,2048]{1,0:T(8,128)(2,1)} %constant.26.clone.gz, bf16[1024,256]{1,0:T(8,128)(2,1)} %constant.23.clone.refs_6_.gy), custom_call_target="tpu_custom_call" | custom-call | tf_op jit(solution)/shard_map/synthesis/pallas_call | solution.py:399
  133.6 0.5 slice_bitcast_fusion.6
  134.2 0.7 reshape.69
  134.8 6.9 %multiply_add_fusion = f32[16,2,16,32,32]{4,3,2,1,0:T(8,128)} fusion(f32[16,16,32]{2,1,0:T(8,128)S(1)} %copy.44, f32[16,2,16,32]{3,2,1,0:T(8,128)S(1)} %copy.49, f32[16,16,32]{2,1,0:T(8,128)S(1)} %copy.43, f32[16,2,16,32]{3,2,1,0:T(8,128)S(1)} %copy.47), kind=kLoop, calls=%fused_computation | loop fusion | flops 1572864 | bytes 2293760 | tf_op jit(solution)/shard_map/add | solution.py:535
  (10 shorter events, 0.2 us)
Async XLA Ops:
  32.4 1.2 copy-start.2
  46.0 0.8 copy-start
  117.8 0.8 copy-start.1
where the time goes:
time: 144 us; the launch traced here: 142 us
  Pallas kernels  112 us (78%)
  other arithmetic  17.3 us (12%)
  local copies, waits for them, and re-layouts  11.8 us (8%)
    pallas_call x3, Pallas kernels, call(): pl.pallas_call(functools.partial(kernel, rows), out_shape=outs, in_specs=...  83 us
    pallas_call x2, Pallas kernels, exchange(): pl.pallas_call(functools.partial(exchange_kernel, n, len(xs), table is no...  28.8 us
    add x1, other arithmetic, shards(): spectral_grad = first * e_r[:, None] + second * e_i[:, None]  6.92 us
    reduce_sum x1, other arithmetic, shards(): u_r = jnp.sum(s_r * w_r - s_i * w_i, axis=2)  5.51 us
    reduce_sum x1, other arithmetic, shards(): m_r = jnp.sum(e_r * w_r + e_i * w_i, axis=3)  4.66 us
    unnamed x7, local copies, waits for them, and re-layouts  2.96 us

commit v1 on v0

--- a/solution.py
+++ b/solution.py
@@ -55,14 +55,16 @@
     block = np.stack([np.stack([zc_low, -zs_low]), np.stack([-zs_low, -zc_low])])
     fz = np.einsum("srzk,ab->aszrbk", block, oct_eye).reshape(OCT * 2 * NZ, 2 * OCT * KZ)
     fz_w = (fz.reshape(-1, KZ) * wz).reshape(fz.shape)
+    fz_k = np.einsum("srzk,ab->aszrkb", block, oct_eye).reshape(fz.shape)
     back = np.stack([np.stack([zc, zs]), np.stack([-zs, zc])])
     gz = np.einsum("rqzk,ab->rakbqz", back, oct_eye).reshape(2 * OCT * KZ, OCT * 2 * NZ)
     gz_w = (np.einsum("rqzk,ab,k->rakbqz", back, oct_eye, wz)).reshape(gz.shape)
+    gz_k = np.einsum("rqzk,ab->rkabqz", back, oct_eye).reshape(gz.shape)
     fx = np.concatenate([xc.T, xs.T], 0).astype(np.float32)
     gx = np.concatenate([xc, xs], 0).astype(np.float32)
     fx2 = np.block([[xc.T, xs.T], [-xs.T, xc.T]]).astype(np.float32)
     gx2 = np.block([[xc, -xs], [xs, xc]]).astype(np.float32)
-    return low(fy), low(gy), low(fz), low(fz_w), low(gz), low(gz_w), fx, gx, fx2, gx2
+    return low(fy), low(gy), low(fz), low(fz_w), low(gz), low(gz_w), fx, gx, fx2, gx2, low(fz_k), low(gz_k)
 
 
 def dot(a, b):
@@ -139,81 +141,6 @@
     )
 
 
-def send_half(n, half, src, dst, send, recv, own):
-    me = lax.axis_index("mp")
-    wide = GLANES * GROUPS // 2
-    lanes = pl.ds(half * wide, wide)
-
-    @pl.loop(1, n)
-    def _(s):
-        peer = lax.rem(me + s, n)
-        remote(
-            src.at[peer, :, lanes],
-            dst.at[me, :, lanes],
-            send.at[half, peer],
-            recv.at[half, me],
-            peer,
-        ).start()
-
-    mine = pltpu.make_async_copy(src.at[me, :, lanes], dst.at[me, :, lanes], own.at[half])
-    mine.start()
-    return mine
-
-
-def wait_half(n, half, src, dst, send, recv):
-    me = lax.axis_index("mp")
-    wide = GLANES * GROUPS // 2
-    lanes = pl.ds(half * wide, wide)
-
-    @pl.loop(1, n)
-    def _(s):
-        peer = lax.rem(me + s, n)
-        both = remote(
-            src.at[peer, :, lanes],
-            dst.at[peer, :, lanes],
-            send.at[half, peer],
-            recv.at[half, peer],
-            peer,
-        )
-        both.wait_recv()
-        both.wait_send()
-
-
-def spread_out(rows, n, field, fy, fz, fx2, spec, src, dst, send, recv, own, ready):
-    mine = []
-    for half in range(2):
-        for g in range(half * GROUPS // 2, (half + 1) * GROUPS // 2):
-            ready(g)
-            res = forward_group(field, g, fy, fz, KY * rows)
-            src[:, :, g * GLANES : (g + 1) * GLANES] = res.reshape(KY, rows, GLANES)
-        if half == 0:
-            pl.semaphore_wait(pltpu.get_barrier_semaphore(), n - 1)
-        mine.append(send_half(n, half, src, dst, send, recv, own))
-    each = GLANES // 2
-    for half in range(2):
-        mine[half].wait()
-        wait_half(n, half, src, dst, send, recv)
-        for g in range(half * GROUPS // 2, (half + 1) * GROUPS // 2):
-            pair = [
-                dst[:, :, g * GLANES + r * each : g * GLANES + (r + 1) * each].reshape(NX, each)
-                for r in range(2)
-            ]
-            spec[:, g * each : (g + 1) * each] = jnp.dot(
-                fx2[...],
-                jnp.concatenate(pair, axis=0),
-                precision=precise,
-                preferred_element_type=F32,
-            )
-
-
-def analysis_kernel(rows, n, feat_hbm, fy, fz, fx2, spec, feat, load, src, dst, send, recv, own):
-    greet(n)
-    loads = load_groups(feat_hbm, feat, load)
-    spread_out(
-        rows, n, feat, fy, fz, fx2, spec, src, dst, send, recv, own, lambda g: loads[g].wait()
-    )
-
-
 def forward_kernel(rows, feat, fy, fz, out):
     plain_forward(feat, fy, fz, out, KY * rows)
 
@@ -244,11 +171,9 @@
 
 
 def middle_kernel(
-    rows, n, feat_hbm, cot_hbm, modes, weight, bias, gz, gy, fy, fz, fx2, pg_hbm, part, sums,
-    field, acc, bacc, kron, feat, cot, pg, fsem, csem, psem, *net,
+    rows, feat_hbm, cot_hbm, modes, weight, bias, gz, gy, fy, fz, pg_hbm, part, sums,
+    field, acc, bacc, kron, feat, cot, pg, fsem, csem, psem,
 ):
-    if net:
-        greet(n)
     loads = load_groups(feat_hbm, feat, fsem) + load_groups(cot_hbm, cot, csem)
     kron[...] = widen(weight[...])
     acc[...] = jnp.zeros_like(acc)
@@ -293,10 +218,7 @@
     by_row = jnp.sum(bacc[...].reshape(C, TILE, NZ), axis=1)
     lane = lax.broadcasted_iota(jnp.int32, (C, LANES), 1)
     sums[...] = pw + jnp.where(lane == C, jnp.sum(by_row, axis=1, keepdims=True), 0.0)
-    if net:
-        spread_out(rows, n, pg, fy, fz, fx2, part, *net, lambda g: None)
-    else:
-        plain_forward(pg, fy, fz, part, KY * rows)
+    plain_forward(pg, fy, fz, part, KY * rows)
     save.wait()
 
 
@@ -327,20 +249,10 @@
         copy.wait()
 
 
-def exchange_kernel(n, arrays, spread, *refs):
+def exchange_kernel(n, arrays, *refs):
     me = lax.axis_index("mp")
     greet(n)
     srcs = refs[:arrays]
-    if spread:
-        table, refs, lines = refs[arrays], refs[:arrays] + refs[arrays + 1 : -1], refs[-1]
-        each = GLANES // 2
-        for g in range(GROUPS):
-            part = srcs[0][:, g * each : (g + 1) * each]
-            both = jnp.dot(table[...], part, precision=precise, preferred_element_type=F32)
-            for r in range(2):
-                at = g * GLANES + r * each
-                lines[:, :, at : at + each] = both[r * NX : (r + 1) * NX].reshape(n, NX // n, each)
-        srcs = (lines, *srcs[1:])
     dsts = refs[arrays : 2 * arrays]
     send, recv, own = refs[2 * arrays :]
     pl.semaphore_wait(pltpu.get_barrier_semaphore(), n - 1)
@@ -369,28 +281,23 @@
             both.wait_send()
 
 
-def exchange(xs, n, cid, table=None):
+def exchange(xs, n, cid):
     shapes = [jax.ShapeDtypeStruct(x.shape, x.dtype) for x in xs]
-    extra = []
-    if table is not None:
-        shapes[0] = jax.ShapeDtypeStruct((n, NX // n, 2 * C * KZ), F32)
-        extra = [table]
     return pl.pallas_call(
-        functools.partial(exchange_kernel, n, len(xs), table is not None),
+        functools.partial(exchange_kernel, n, len(xs)),
         out_shape=shapes,
-        in_specs=[VMEM] * (len(xs) + len(extra)),
+        in_specs=[VMEM] * len(xs),
         out_specs=[VMEM] * len(xs),
         scratch_shapes=[
             pltpu.SemaphoreType.DMA((len(xs), n)),
             pltpu.SemaphoreType.DMA((len(xs), n)),
             pltpu.SemaphoreType.DMA((len(xs),)),
-        ]
-        + [pltpu.VMEM(shapes[0].shape, F32)] * len(extra),
+        ],
         compiler_params=pltpu.CompilerParams(
             collective_id=cid, has_side_effects=True, vmem_limit_bytes=16 << 20
         ),
         name=f"exchange{cid}",
-    )(*xs, *extra)
+    )(*xs)
 
 
 def call(kernel, rows, outs, scratch, args, name, far=(), far_out=(), cid=None):
@@ -440,19 +347,440 @@
     return lines.reshape(n, rows, -1)
 
 
-def split_modes(spec):
-    v = jnp.transpose(spec.reshape(2, KX, C, KZ), (0, 3, 1, 2))
-    return v[0], v[1]
-
-
-def join_modes(real, imag):
-    return jnp.transpose(jnp.stack([real, imag]), (0, 2, 3, 1)).reshape(2 * KX, C * KZ)
+HALF = OCT * KZ
+FULL = 2 * KX * C
+ONE = 1.0 / SCALE
+RING = 4
+PAIR = 2 * NZ
+CHUNK = 256
+SUB = 128
+ROOT = math.sqrt(2.0 / math.pi)
+
+
+def sharp(a, b):
+    return jnp.dot(a, b, precision=precise, preferred_element_type=F32)
+
+
+def lane_weight():
+    k = lax.broadcasted_iota(jnp.int32, (1, GLANES), 1) % HALF // OCT
+    return jnp.where(k == 0, SCALE, 2.0 * SCALE)
+
+
+def send_group(n, turn, g, src, dst, send, recv):
+    me = lax.axis_index("mp")
+
+    @pl.loop(1, n)
+    def _(s):
+        peer = lax.rem(me + s, n)
+        remote(src.at[g, peer], dst.at[g, me], send.at[turn, g], recv.at[turn, g], peer).start()
+
+    pltpu.make_async_copy(src.at[g, me], dst.at[g, me], recv.at[turn, g]).start()
+
+
+def wait_bytes(ref, sem):
+    pltpu.make_async_copy(ref, ref, sem).wait()
+
+
+def wait_sent(n, turn, g, src, send):
+    wait_bytes(src.at[g, pl.ds(0, n - 1)], send.at[turn, g])
+
+
+def spectrum(dst, g, fx2):
+    pair = [dst[g, :, :, r * HALF : (r + 1) * HALF].reshape(NX, HALF) for r in range(2)]
+    return sharp(fx2[...], jnp.concatenate(pair, axis=0))
+
+
+def gather_channels(parts, k):
+    lane = lax.broadcasted_iota(jnp.int32, (2 * KX, LANES), 1) // OCT
+    out = jnp.zeros((2 * KX, LANES), F32)
+    for g in range(GROUPS):
+        shift = (g * OCT - k * OCT) % LANES
+        moved = pltpu.roll(parts[g], shift, 1) if shift else parts[g]
+        out = jnp.where(lane == g, moved, out)
+    return out
+
+
+def fill_lanes(v):
+    v = v + pltpu.roll(v, C, 1)
+    return v + pltpu.roll(v, 2 * C, 1)
+
+
+def own_mode(m):
+    row = lax.broadcasted_iota(jnp.int32, (2 * KX, LANES), 0) % KX
+    lane = lax.broadcasted_iota(jnp.int32, (2 * KX, LANES), 1) // C
+    return row == m * (LANES // C) + lane
+
+
+def diagonal(spread):
+    turned = jnp.concatenate([-spread[KX:], spread[:KX]], axis=0)
+    blocks = [jnp.where(own_mode(m), v, 0.0) for v in (spread, turned) for m in range(KX * C // LANES)]
+    return jnp.concatenate(blocks, axis=1)
+
+
+def put_channels(parts, k, v):
+    lane = lax.broadcasted_iota(jnp.int32, (2 * KX, LANES), 1) // OCT
+    for g in range(GROUPS):
+        shift = (k * OCT - g * OCT) % LANES
+        moved = pltpu.roll(v, shift, 1) if shift else v
+        parts[g] = jnp.where(lane == k, moved, parts[g])
+
+
+def lines_out(parts, gx2, src, n):
+    for g in range(GROUPS):
+        both = sharp(gx2[...], parts[g])
+        for r in range(2):
+            src[g, :, :, r * HALF : (r + 1) * HALF] = both[r * NX : (r + 1) * NX].reshape(
+                n, NX // n, HALF
+            )
+
+
+def widen_with(weight, turn):
+    n = C * TILE
+    row = lax.broadcasted_iota(jnp.int32, (n, C), 0) // TILE
+    up = jnp.where(row == lax.broadcasted_iota(jnp.int32, (n, C), 1), 1.0, 0.0).astype(BF)
+    dims = (((1,), (1 if turn else 0,)), ((), ()))
+    left = lax.dot_general(up, weight, dims, preferred_element_type=F32).astype(BF)
+    full = lax.dot_general(left, up, (((1,), (1,)), ((), ())), preferred_element_type=F32)
+    ri = lax.broadcasted_iota(jnp.int32, (n, n), 0)
+    ci = lax.broadcasted_iota(jnp.int32, (n, n), 1)
+    return jnp.where(ri % TILE == ci % TILE, full, 0.0).astype(BF)
+
+
+def slope(x):
+    x2 = x * x
+    th = jnp.tanh(x * (ROOT + (ROOT * 0.044715) * x2))
+    return (1.0 + th) * (0.5 + (1.0 - th) * (x * (0.5 * ROOT + (1.5 * ROOT * 0.044715) * x2)))
+
+
+def unfold(lhs, gz, ub):
+    lines = lhs.shape[0]
+    u = dot(lhs, gz[...]).astype(BF)
+    for q in range(OCT):
+        for r in range(2):
+            at = (2 * q + r) * NZ
+            ub[r * lines : (r + 1) * lines, q * NZ : (q + 1) * NZ] = u[:, at : at + NZ]
+
+
+def heart_kernel(
+    rows, n, feat_hbm, cot_hbm, w_hbm, fy_hbm, fz_hbm, gy_hbm, gz_hbm, weight, bias, fx2, gx2,
+    mix_hbm, back, vout, dout, total,
+    feat, cot, pg, field, ring, wb, fy, fz, gy, gz, kron, acc, ub, stage, src_a, src_b,
+    dst_1, dst_2, dst_3, dst_4, sums, every, fsem, csem, tsem, wsem, send, recv, ssem, rsem, osem,
+):
+    me = lax.axis_index("mp")
+    cells = rows * NY
+    lines = KY * rows
+    steps = cells // (STEP * TILE)
+    greet(n)
+    early = [pltpu.make_async_copy(a, b, tsem.at[i]) for i, (a, b) in enumerate(((fy_hbm, fy), (fz_hbm, fz)))]
+    late = [pltpu.make_async_copy(a, b, tsem.at[2 + i]) for i, (a, b) in enumerate(((gy_hbm, gy), (gz_hbm, gz)))]
+
+    def feat_copy(g):
+        part = pl.ds(g * OCT, OCT)
+        return pltpu.make_async_copy(feat_hbm.at[part], feat.at[part], fsem.at[g])
+
+    def cot_copy(g):
+        part = pl.ds(g * OCT, OCT)
+        return pltpu.make_async_copy(cot_hbm.at[part], cot.at[part], csem.at[g])
+
+    def ring_copy(k, slot):
+        return pltpu.make_async_copy(w_hbm.at[k], ring.at[slot], wsem.at[slot])
+
+    for copy in early:
+        copy.start()
+    for g in range(GROUPS):
+        feat_copy(g).start()
+    for copy in early:
+        copy.wait()
+
+    @pl.loop(0, GROUPS)
+    def _(g):
+        feat_copy(g).wait()
+        res = forward_group(feat, g, fy, fz, lines)
+        src_a[g] = res.reshape(n, rows, GLANES)
+
+        @pl.when(g == 0)
+        def _():
+            pl.semaphore_wait(pltpu.get_barrier_semaphore(), n - 1)
+
+        send_group(n, 0, g, src_a, dst_1, send, recv)
+
+    for k in range(RING):
+        ring_copy(k, k).start()
+    for copy in late:
+        copy.start()
+    for g in range(GROUPS):
+        cot_copy(g).start()
+
+    kron[...] = widen_with(weight[...], False)
+    size = C * TILE
+    row = lax.broadcasted_iota(jnp.int32, (size, C), 0) // TILE
+    column = jnp.where(row == lax.broadcasted_iota(jnp.int32, (size, C), 1), bias[...], 0.0)
+    shift = jnp.sum(column, axis=1, keepdims=True)
+
+    @pl.loop(0, steps)
+    def _(s):
+        f = jnp.concatenate([tile_of(feat, STEP * s + h) for h in range(STEP)], axis=1)
+        mix = dot(kron[...], f)
+        for h in range(STEP):
+            put_tile(field, STEP * s + h, mix[:, h * NZ : (h + 1) * NZ] + shift)
+
+    @pl.loop(0, KZ // RING)
+    def _(i):
+        for slot in range(RING):
+            k = i * RING + slot
+            ring_copy(k, slot).wait()
+            wb[k] = ring[slot].astype(BF)
+
+            @pl.when(k + RING < KZ)
+            def _():
+                ring_copy(k + RING, slot).start()
+
+    for g in range(GROUPS):
+        wait_bytes(dst_1.at[g], recv.at[0, g])
+        vout[g] = spectrum(dst_1, g, fx2)
+    parts = [vout[g] for g in range(GROUPS)]
+    mixed = [jnp.zeros((2 * KX, LANES), F32) for _ in range(GROUPS)]
+    for k in range(KZ):
+        left = diagonal(fill_lanes(gather_channels(parts, k))).astype(BF)
+        stage[k, :, :C] = dot(left, wb[k])
+    for k in range(KZ):
+        put_channels(mixed, k, stage[k])
+    lines_out(mixed, gx2, src_b, n)
+    for g in range(GROUPS):
+        send_group(n, 1, g, src_b, dst_2, send, recv)
+    for copy in late:
+        copy.wait()
+    for g in range(GROUPS):
+        wait_sent(n, 0, g, src_a, send)
+        cot_copy(g).wait()
+
+    @pl.loop(0, GROUPS)
+    def _(g):
+        wait_bytes(dst_2.at[g], recv.at[1, g])
+        lhs = (dst_2[g].reshape(lines, GLANES) * lane_weight()).astype(BF)
+        unfold(lhs, gz, ub)
+
+        @pl.loop(0, OCT // 2)
+        def _(p):
+            uv = ub[:, pl.ds(pl.multiple_of(p * PAIR, PAIR), PAIR)]
+            for r in range(0, cells, CHUNK):
+                res = dot(gy[r : r + CHUNK, :], uv)
+                for h in range(2):
+                    c = g * OCT + 2 * p + h
+                    for t in range(0, CHUNK, SUB):
+                        at = slice(r + t, r + t + SUB)
+                        x = res[t : t + SUB, h * NZ : (h + 1) * NZ] + field[c, at]
+                        pg[c, at] = (cot[c, at].astype(F32) * slope(x)).astype(BF)
+
+        out = forward_group(pg, g, fy, fz, lines) * lane_weight()
+        src_a[g] = out.reshape(n, rows, GLANES)
+        send_group(n, 2, g, src_a, dst_3, send, recv)
+
+    acc[...] = jnp.zeros_like(acc)
+
+    @pl.loop(0, steps)
+    def _(s):
+        f = jnp.concatenate([tile_of(feat, STEP * s + h) for h in range(STEP)], axis=1)
+        g = jnp.concatenate([tile_of(pg, STEP * s + h) for h in range(STEP)], axis=1)
+        acc[...] += lax.dot_general(g, f, (((1,), (1,)), ((), ())), preferred_element_type=F32)
+
+    ri = lax.broadcasted_iota(jnp.int32, (size, size), 0)
+    ci = lax.broadcasted_iota(jnp.int32, (size, size), 1)
+    masked = jnp.where(ri % TILE == ci % TILE, acc[...], 0.0)
+    rows_sum = jnp.sum(masked.reshape(C, TILE, size), axis=1)
+    fold = jnp.where(
+        lax.broadcasted_iota(jnp.int32, (size, LANES), 0) // TILE
+        == lax.broadcasted_iota(jnp.int32, (size, LANES), 1),
+        1.0,
+        0.0,
+    ).astype(F32)
+    pw = sharp(rows_sum, fold)
+    packed = pw[:8]
+    for i in range(1, C // 8):
+        packed = packed + pltpu.roll(pw[8 * i : 8 * i + 8], i * C, 1)
+    sums[:8] = packed
+    kron[...] = widen_with(weight[...], True)
+
+    for g in range(GROUPS):
+        wait_bytes(dst_3.at[g], recv.at[2, g])
+        dout[g] = spectrum(dst_3, g, fx2)
+    parts = [dout[g] for g in range(GROUPS)]
+    dc = jnp.zeros((1, LANES), F32)
+    lane = lax.broadcasted_iota(jnp.int32, (1, LANES), 1)
+    for g in range(GROUPS):
+        v = parts[g][KX // 2 : KX // 2 + 1]
+        v = pltpu.roll(v, g * OCT, 1) if g else v
+        dc = jnp.where(lane // OCT == g, v * ONE, dc)
+    owner = jnp.where(me == KY // 2, 1.0, 0.0)
+    first = lax.broadcasted_iota(jnp.int32, (8, LANES), 0) == 0
+    sums[8:] = jnp.where(first, dc * owner, 0.0)
+    mixed = [jnp.zeros((2 * KX, LANES), F32) for _ in range(GROUPS)]
+    half = KX * C
+    for k in range(KZ):
+        d = gather_channels(parts, k)[:, :C].astype(BF)
+        full = lax.dot_general(d, wb[k], (((1,), (1,)), ((), ())), preferred_element_type=F32)
+        a0 = jnp.zeros((2 * KX, LANES), F32)
+        a1 = a0
+        for m in range(half // LANES):
+            own = own_mode(m)
+            a0 = a0 + jnp.where(own, full[:, m * LANES : (m + 1) * LANES], 0.0)
+            a1 = a1 + jnp.where(own, full[:, half + m * LANES : half + (m + 1) * LANES], 0.0)
+        both = a0 + jnp.concatenate([a1[KX:], -a1[:KX]], axis=0)
+        put_channels(mixed, k, fill_lanes(both))
+    for g in range(GROUPS):
+        wait_sent(n, 1, g, src_b, send)
+    lines_out(mixed, gx2, src_b, n)
+    for g in range(GROUPS):
+        send_group(n, 3, g, src_b, dst_4, send, recv)
+
+    @pl.loop(1, n)
+    def _(s):
+        peer = lax.rem(me + s, n)
+        remote(sums, every.at[me], ssem, rsem, peer).start()
+
+    pltpu.make_async_copy(sums, every.at[me], rsem).start()
+
+    @pl.loop(0, steps)
+    def _(s):
+        f = jnp.concatenate([tile_of(pg, STEP * s + h) for h in range(STEP)], axis=1)
+        mix = dot(kron[...], f)
+        for h in range(STEP):
+            put_tile(cot, STEP * s + h, mix[:, h * NZ : (h + 1) * NZ].astype(BF))
+
+    save = pltpu.make_async_copy(cot, mix_hbm, osem)
+    save.start()
+    for g in range(GROUPS):
+        wait_bytes(dst_4.at[g], recv.at[3, g])
+        back[g] = dst_4[g].reshape(lines, GLANES).astype(BF)
+    wait_bytes(every, rsem)
+    total[...] = jnp.sum(every[...], axis=0) * float(NX * NY * NZ) ** (-0.5)
+    wait_bytes(every.at[pl.ds(0, n - 1)], ssem)
+    for g in range(GROUPS):
+        wait_sent(n, 2, g, src_a, send)
+        wait_sent(n, 3, g, src_b, send)
+    save.wait()
+
+
+def tail_kernel(
+    rows, mix_hbm, gz_hbm, gy_hbm, back, v, d, total, grad_hbm, sg_hbm, pwg, bg,
+    mix, out, gz, gy, ub, sg, msem, tsem, osem, ssem,
+):
+    cells = rows * NY
+    tables_in = [pltpu.make_async_copy(a, b, tsem.at[i]) for i, (a, b) in enumerate(((gz_hbm, gz), (gy_hbm, gy)))]
+    for copy in tables_in:
+        copy.start()
+    loads = load_groups(mix_hbm, mix, msem)
+    t = total[...]
+    for i in range(C // 8):
+        part = pltpu.roll(t[:8], LANES - i * C, 1) if i else t[:8]
+        pwg[8 * i : 8 * i + 8, :] = part[:, :C]
+    bg[...] = t[8:9, :C]
+    vs = [v[g] for g in range(GROUPS)]
+    ds = [d[g] for g in range(GROUPS)]
+    for k in range(KZ):
+        full = diagonal(fill_lanes(gather_channels(vs, k)))
+        right = gather_channels(ds, k)[:, :C]
+        high, top = full.astype(BF), right.astype(BF)
+        rest, low_part = (full - high.astype(F32)).astype(BF), (right - top.astype(F32)).astype(BF)
+        left = jnp.concatenate([high, rest, high], axis=0)
+        side = jnp.concatenate([top, top, low_part], axis=0)
+        sg[k] = lax.dot_general(left, side, (((0,), (0,)), ((), ())), preferred_element_type=F32)
+        pltpu.make_async_copy(sg.at[k], sg_hbm.at[k], ssem.at[k]).start()
+    for copy in tables_in:
+        copy.wait()
+    for g in range(GROUPS):
+        loads[g].wait()
+        unfold(back[g], gz, ub)
+
+        @pl.loop(0, OCT // 2)
+        def _(p):
+            uv = ub[:, pl.ds(pl.multiple_of(p * PAIR, PAIR), PAIR)]
+            for r in range(0, cells, CHUNK):
+                res = dot(gy[r : r + CHUNK, :], uv)
+                for h in range(2):
+                    c = g * OCT + 2 * p + h
+                    at = slice(r, r + CHUNK)
+                    out[c, at] = (res[:, h * NZ : (h + 1) * NZ] + mix[c, at].astype(F32)).astype(BF)
+
+        part = pl.ds(g * OCT, OCT)
+        pltpu.make_async_copy(out.at[part], grad_hbm.at[part], osem.at[g]).start()
+    for g in range(GROUPS):
+        part = pl.ds(g * OCT, OCT)
+        pltpu.make_async_copy(out.at[part], grad_hbm.at[part], osem.at[g]).wait()
+    for k in range(KZ):
+        pltpu.make_async_copy(sg.at[k], sg_hbm.at[k], ssem.at[k]).wait()
+
+
+def fused_shards(n, rows, features, cotangent, spectral_weight, pointwise_weight, biases):
+    known = tables(rows)
+    fy, gy, fx2, gx2, fz, gz = [jnp.asarray(known[i]) for i in (0, 1, 8, 9, 10, 11)]
+    cells = rows * NY
+    lines = KY * rows
+    dma = pltpu.SemaphoreType.DMA
+    block = pltpu.VMEM((C, cells, NZ), BF)
+    shape = jax.ShapeDtypeStruct
+    wide = C * TILE
+    swap = pltpu.VMEM((GROUPS, n, rows, GLANES), F32)
+    spec = shape((GROUPS, 2 * KX, LANES), F32)
+    mix, back, v, d, total = pl.pallas_call(
+        functools.partial(heart_kernel, rows, n),
+        out_shape=[
+            shape((C, cells, NZ), BF), shape((GROUPS, lines, GLANES), BF), spec, spec,
+            shape((16, LANES), F32),
+        ],
+        in_specs=[HBM] * 7 + [VMEM] * 4,
+        out_specs=[HBM] + [VMEM] * 4,
+        scratch_shapes=[
+            block, block, block, pltpu.VMEM((C, cells, NZ), F32),
+            pltpu.VMEM((RING, FULL, C), F32), pltpu.VMEM((KZ, FULL, C), BF),
+            pltpu.VMEM(fy.shape, BF), pltpu.VMEM(fz.shape, BF),
+            pltpu.VMEM(gy.shape, BF), pltpu.VMEM(gz.shape, BF),
+            pltpu.VMEM((wide, wide), BF), pltpu.VMEM((wide, wide), F32),
+            pltpu.VMEM((2 * lines, OCT * NZ), BF), pltpu.VMEM((KZ, 2 * KX, LANES), F32),
+            swap, swap, swap, swap, swap, swap,
+            pltpu.VMEM((16, LANES), F32), pltpu.VMEM((n, 16, LANES), F32),
+            dma((GROUPS,)), dma((GROUPS,)), dma((4,)), dma((RING,)),
+            dma((4, GROUPS)), dma((4, GROUPS)), dma, dma, dma,
+        ],
+        compiler_params=pltpu.CompilerParams(
+            collective_id=1, has_side_effects=True, vmem_limit_bytes=62 << 20
+        ),
+        name="heart",
+    )(
+        features.reshape(C, cells, NZ), cotangent.reshape(C, cells, NZ),
+        spectral_weight.reshape(KZ, FULL, C), fy, fz, gy, gz, pointwise_weight,
+        biases.reshape(1, C), fx2, gx2,
+    )
+    grad, sg, pwg, bg = pl.pallas_call(
+        functools.partial(tail_kernel, rows),
+        out_shape=[
+            shape((C, cells, NZ), BF), shape((KZ, FULL, C), F32), shape((C, C), F32),
+            shape((1, C), F32),
+        ],
+        in_specs=[HBM] * 3 + [VMEM] * 4,
+        out_specs=[HBM, HBM, VMEM, VMEM],
+        scratch_shapes=[
+            block, block, pltpu.VMEM(gz.shape, BF), pltpu.VMEM(gy.shape, BF),
+            pltpu.VMEM((2 * lines, OCT * NZ), BF), pltpu.VMEM((KZ, FULL, C), F32),
+            dma((GROUPS,)), dma((2,)), dma((GROUPS,)), dma((KZ,)),
+        ],
+        compiler_params=pltpu.CompilerParams(vmem_limit_bytes=56 << 20),
+        name="tail",
+    )(mix, gz, gy, back, v, d, total)
+    return (
+        grad.reshape(features.shape), sg.reshape(spectral_weight.shape), pwg, bg.reshape(C),
+    )
 
 
 def shards(features, cotangent, spectral_weight, pointwise_weight, biases):
     n = lax.axis_size("mp")
     rows = NX // n
-    fy, gy, fz, fz_w, gz, gz_w, fx, gx, fx2, gx2 = [jnp.asarray(t) for t in tables(rows)]
+    if n == KY:
+        return fused_shards(
+            n, rows, features, cotangent, spectral_weight, pointwise_weight, biases
+        )
+    fy, gy, fz, fz_w, gz, gz_w, fx, gx = [jnp.asarray(t) for t in tables(rows)[:8]]
     cells = rows * NY
     feat = features.reshape(C, cells, NZ)
     cot = cotangent.reshape(C, cells, NZ)
@@ -464,35 +792,15 @@
     wide = C * TILE
     dma = pltpu.SemaphoreType.DMA
     sems = dma((GROUPS,))
-    fused = n == KY
-    lines = pltpu.VMEM((n, rows, 2 * C * KZ), F32)
-    net = [lines, lines, dma((2, n)), dma((2, n)), dma((2,))] if fused else []
-    if fused:
-        spread = jax.ShapeDtypeStruct((2 * KX, C * KZ), F32)
-        spec = call(
-            lambda r, *refs: analysis_kernel(r, n, *refs),
-            rows,
-            [spread],
-            [block, sems, *net],
-            (feat, fy, fz, fx2),
-            "analysis",
-            far=(0,),
-            cid=1,
-        )[0]
-        v_r, v_i = split_modes(spec)
-    else:
-        part = call(forward_kernel, rows, [spread], [], (feat, fy, fz), "analysis")[0]
-        v_r, v_i = lines_forward(exchange([owner_blocks(part, n, rows)], n, 1)[0], fx)
+    part = call(forward_kernel, rows, [spread], [], (feat, fy, fz), "analysis")[0]
+    v_r, v_i = lines_forward(exchange([owner_blocks(part, n, rows)], n, 1)[0], fx)
     w_r, w_i = spectral_weight[:, 0], spectral_weight[:, 1]
     s_r, s_i = v_r[..., None], v_i[..., None]
     u_r = jnp.sum(s_r * w_r - s_i * w_i, axis=2)
     u_i = jnp.sum(s_r * w_i + s_i * w_r, axis=2)
-    if fused:
-        modes = exchange([join_modes(u_r, u_i)], n, 2, gx2)[0]
-    else:
-        modes = exchange([lines_back(u_r, u_i, gx, n, rows)], n, 2)[0]
+    modes = exchange([lines_back(u_r, u_i, gx, n, rows)], n, 2)[0]
     pg, dpart, sums = call(
-        lambda r, *refs: middle_kernel(r, n, *refs),
+        middle_kernel,
         rows,
         [whole, spread, jax.ShapeDtypeStruct((C, LANES), F32)],
         [
@@ -506,18 +814,13 @@
             sems,
             sems,
             dma,
-            *net,
         ],
-        (feat, cot, plane_blocks(modes, n, rows), pointwise_weight, bias, gz_w, gy, fy, fz_w, fx2),
+        (feat, cot, plane_blocks(modes, n, rows), pointwise_weight, bias, gz_w, gy, fy, fz_w),
         "middle",
         far=(0, 1),
         far_out=(0,),
-        cid=3 if fused else None,
     )
-    if fused:
-        d_r, d_i = split_modes(dpart)
-    else:
-        d_r, d_i = lines_forward(exchange([owner_blocks(dpart, n, rows)], n, 3)[0], fx)
+    d_r, d_i = lines_forward(exchange([owner_blocks(dpart, n, rows)], n, 3)[0], fx)
     e_r, e_i = d_r[:, :, None, :], d_i[:, :, None, :]
     m_r = jnp.sum(e_r * w_r + e_i * w_i, axis=3)
     m_i = jnp.sum(e_i * w_r - e_r * w_i, axis=3)
@@ -525,10 +828,7 @@
         [sums[:, :C].reshape(-1, LANES), jnp.pad(sums[:, C], (0, LANES - C))[None]], axis=0
     )
     mine = jnp.broadcast_to(packed, (n, *packed.shape))
-    if fused:
-        back, every = exchange([join_modes(m_r, m_i), mine], n, 4, gx2)
-    else:
-        back, every = exchange([lines_back(m_r, m_i, gx, n, rows), mine], n, 4)
+    back, every = exchange([lines_back(m_r, m_i, gx, n, rows), mine], n, 4)
     total = jnp.sum(every, axis=0)
     first = jnp.stack([v_r, -v_i], axis=1)[..., None]
     second = jnp.stack([v_i, v_r], axis=1)[..., None]
@@ -537,7 +837,7 @@
         last_kernel,
         rows,
         [whole],
-        [field, pltpu.VMEM((wide, wide), BF), block, block, sems, pltpu.SemaphoreType.DMA((SAVES,))],
+        [field, pltpu.VMEM((wide, wide), BF), block, block, sems, dma((SAVES,))],
         (pg, plane_blocks(back, n, rows), pointwise_weight.T, gz, gy),
         "synthesis",
         far=(0,),

time: 144 us -> 96.4 us (0.67); the launches traced: 142 us -> 96.2 us
  other arithmetic: 17.3 us -> 0 us
  Pallas kernels: 112 us -> 95.6 us
  local copies, waits for them, and re-layouts: 11.8 us -> 0 us
    pallas_call x5 -> x2, Pallas kernels: 112 us -> 95.6 us  [the longest x1 78.4 us: fused_shards(): pl.pallas_call(functools.partial(heart_kernel, rows, n), out_shape=[shape...]
    reduce_sum x3 -> x0, other arithmetic: 10.2 us -> none  [the longest x1 5.51 us: shards(): u_r = jnp.sum(s_r * w_r - s_i * w_i, axis=2)]
    add x1 -> x0, other arithmetic: 6.92 us -> none  [shards(): spectral_grad = first * e_r[:, None] + second * e_i[:, None]]
    reshape x6 -> x0, local copies, waits for them, and re-layouts: 4.09 us -> none  [the longest x2 2.08 us: split_modes(): v = jnp.transpose(spec.reshape(2, KX, C, KZ), (0, 3, 1, 2))]
    unnamed x7 -> x0, local copies, waits for them, and re-layouts: 2.96 us -> none
where the time goes in v1:
time: 96.4 us; the launch traced here: 96.2 us
  Pallas kernels  95.6 us (99%)
    pallas_call x1, Pallas kernels, fused_shards(): pl.pallas_call(functools.partial(heart_kernel, rows, n), out_shape=[shape...  78.4 us
    pallas_call x1, Pallas kernels, fused_shards(): pl.pallas_call(functools.partial(tail_kernel, rows), out_shape=[shape((C,...  17.2 us

profile of v1, /device:TPU:0, one launch (start us, length us, event | category | flops | bytes accessed | tf_op | source)
XLA Modules:
  0.0 96.2 jit_solution(18207826748302851923)
XLA Ops:
  0.6 78.4 %heart.1 = (bf16[32,1024,128]{2,1,0:T(8,128)(2,1)}, bf16[4,128,256]{2,1,0:T(8,128)(2,1)}, f32[4,32,128]{2,1,0:T(8,128)}, f32[4,32,128]{2,1,0:T(8,128)}, f32[16,128]{1,0:T(8,128)}) custom-call(bf16[32,1024,128]{2,1,0:T(8,128)(2,1)} %bitcast.7, bf16[32,1024,128]{2,1,0:T(8,128)(2,1)} %bitcast.8, f32[16,1024,32]{2,1,0:T(8,128)} %bitcast.9, ...), custom_call_target="tpu_custom_call" | custom-call | tf_op jit(solution)/shard_map/heart/pallas_call | solution.py:726
  79.1 17.2 %tail.1 = (bf16[32,1024,128]{2,1,0:T(8,128)(2,1)}, f32[16,1024,32]{2,1,0:T(8,128)}, f32[32,32]{1,0:T(8,128)}, f32[1,32]{1,0:T(1,128)}) custom-call(bf16[32,1024,128]{2,1,0:T(8,128)(2,1)} %get-tuple-element.13.mix_hbm, bf16[256,2048]{1,0:T(8,128)(2,1)} %constant.17.clone.gz_hbm, bf16[1024,256]{1,0:T(8,128)(2,1)} %constant.13.clone.gy_hbm, ...), custom_call_target="tpu_custom_call" | custom-call | tf_op jit(solution)/shard_map/tail/pallas_call | solution.py:755

commit v2 on v1

--- a/solution.py
+++ b/solution.py
@@ -55,6 +55,7 @@
     block = np.stack([np.stack([zc_low, -zs_low]), np.stack([-zs_low, -zc_low])])
     fz = np.einsum("srzk,ab->aszrbk", block, oct_eye).reshape(OCT * 2 * NZ, 2 * OCT * KZ)
     fz_w = (fz.reshape(-1, KZ) * wz).reshape(fz.shape)
+    fy_k = np.einsum("syj,xw->sxjwy", np.stack([yc, ys]), np.eye(2)).reshape(4 * KY, 2 * NY)
     fz_k = np.einsum("srzk,ab->aszrkb", block, oct_eye).reshape(fz.shape)
     back = np.stack([np.stack([zc, zs]), np.stack([-zs, zc])])
     gz = np.einsum("rqzk,ab->rakbqz", back, oct_eye).reshape(2 * OCT * KZ, OCT * 2 * NZ)
@@ -64,7 +65,7 @@
     gx = np.concatenate([xc, xs], 0).astype(np.float32)
     fx2 = np.block([[xc.T, xs.T], [-xs.T, xc.T]]).astype(np.float32)
     gx2 = np.block([[xc, -xs], [xs, xc]]).astype(np.float32)
-    return low(fy), low(gy), low(fz), low(fz_w), low(gz), low(gz_w), fx, gx, fx2, gx2, low(fz_k), low(gz_k)
+    return low(fy), low(gy), low(fz), low(fz_w), low(gz), low(gz_w), fx, gx, fx2, gx2, low(fz_k), low(gz_k), low(fy_k)
 
 
 def dot(a, b):
@@ -350,9 +351,11 @@
 HALF = OCT * KZ
 FULL = 2 * KX * C
 ONE = 1.0 / SCALE
-RING = 4
+RING = 8
+EIGHT = 8
+BATCH = 16
 PAIR = 2 * NZ
-CHUNK = 256
+DUO = 2 * NY
 SUB = 128
 ROOT = math.sqrt(2.0 / math.pi)
 
@@ -434,22 +437,62 @@
             )
 
 
+def halves(ref, t):
+    v = tile_of(ref, t).reshape(C, TILE, NZ).astype(F32)
+    return [
+        v[:, w * EIGHT : (w + 1) * EIGHT].reshape(C * EIGHT, NZ).astype(BF)
+        for w in range(TILE // EIGHT)
+    ]
+
+
+def batch_of(ref, s):
+    return jnp.concatenate([v for h in range(BATCH) for v in halves(ref, BATCH * s + h)], axis=1)
+
+
+def unbatch(mix, h):
+    return [
+        mix[:, (2 * h + w) * NZ : (2 * h + w + 1) * NZ].reshape(C, EIGHT, NZ) for w in range(2)
+    ]
+
+
 def widen_with(weight, turn):
-    n = C * TILE
-    row = lax.broadcasted_iota(jnp.int32, (n, C), 0) // TILE
+    n = C * EIGHT
+    row = lax.broadcasted_iota(jnp.int32, (n, C), 0) // EIGHT
     up = jnp.where(row == lax.broadcasted_iota(jnp.int32, (n, C), 1), 1.0, 0.0).astype(BF)
     dims = (((1,), (1 if turn else 0,)), ((), ()))
     left = lax.dot_general(up, weight, dims, preferred_element_type=F32).astype(BF)
     full = lax.dot_general(left, up, (((1,), (1,)), ((), ())), preferred_element_type=F32)
     ri = lax.broadcasted_iota(jnp.int32, (n, n), 0)
     ci = lax.broadcasted_iota(jnp.int32, (n, n), 1)
-    return jnp.where(ri % TILE == ci % TILE, full, 0.0).astype(BF)
+    return jnp.where(ri % EIGHT == ci % EIGHT, full, 0.0).astype(BF)
 
 
 def slope(x):
     x2 = x * x
     th = jnp.tanh(x * (ROOT + (ROOT * 0.044715) * x2))
     return (1.0 + th) * (0.5 + (1.0 - th) * (x * (0.5 * ROOT + (1.5 * ROOT * 0.044715) * x2)))
+
+
+def fold_pair(outs):
+    parts = []
+    for h in range(2):
+        for s in range(2):
+            rows = [
+                o[s * 2 * KY : (s + 1) * 2 * KY, h * NZ : (h + 1) * NZ] for o in outs
+            ]
+            parts.append(jnp.concatenate(rows, axis=0))
+    return parts
+
+
+def put_plane(parts, fz, weight, tmp, src, g, rows):
+    res = dot(jnp.concatenate(parts, axis=1), fz[...])
+    if weight is not None:
+        res = res * weight
+    for r in range(2):
+        tmp[r] = res[:, r * HALF : (r + 1) * HALF]
+    for j in range(KY):
+        for r in range(2):
+            src[g, j, :, r * HALF : (r + 1) * HALF] = tmp[r, pl.ds(j, rows, stride=KY), :]
 
 
 def unfold(lhs, gz, ub):
@@ -465,12 +508,13 @@
     rows, n, feat_hbm, cot_hbm, w_hbm, fy_hbm, fz_hbm, gy_hbm, gz_hbm, weight, bias, fx2, gx2,
     mix_hbm, back, vout, dout, total,
     feat, cot, pg, field, ring, wb, fy, fz, gy, gz, kron, acc, ub, stage, src_a, src_b,
-    dst_1, dst_2, dst_3, dst_4, sums, every, fsem, csem, tsem, wsem, send, recv, ssem, rsem, osem,
+    dst_1, dst_2, dst_3, dst_4, sums, every, tmp, fsem, csem, tsem, wsem, send, recv, ssem, rsem, osem,
 ):
     me = lax.axis_index("mp")
     cells = rows * NY
     lines = KY * rows
-    steps = cells // (STEP * TILE)
+    steps = cells // (BATCH * TILE)
+    duos = cells // DUO
     greet(n)
     early = [pltpu.make_async_copy(a, b, tsem.at[i]) for i, (a, b) in enumerate(((fy_hbm, fy), (fz_hbm, fz)))]
     late = [pltpu.make_async_copy(a, b, tsem.at[2 + i]) for i, (a, b) in enumerate(((gy_hbm, gy), (gz_hbm, gz)))]
@@ -496,8 +540,16 @@
     @pl.loop(0, GROUPS)
     def _(g):
         feat_copy(g).wait()
-        res = forward_group(feat, g, fy, fz, lines)
-        src_a[g] = res.reshape(n, rows, GLANES)
+        parts = []
+        for q in range(0, OCT, 2):
+            c = g * OCT + q
+            outs = []
+            for x in range(duos):
+                at = slice(x * DUO, (x + 1) * DUO)
+                both = jnp.concatenate([feat[c, at], feat[c + 1, at]], axis=1)
+                outs.append(dot(fy[...], both).astype(BF))
+            parts += fold_pair(outs)
+        put_plane(parts, fz, None, tmp, src_a, g, rows)
 
         @pl.when(g == 0)
         def _():
@@ -513,17 +565,18 @@
         cot_copy(g).start()
 
     kron[...] = widen_with(weight[...], False)
-    size = C * TILE
-    row = lax.broadcasted_iota(jnp.int32, (size, C), 0) // TILE
+    size = C * EIGHT
+    row = lax.broadcasted_iota(jnp.int32, (size, C), 0) // EIGHT
     column = jnp.where(row == lax.broadcasted_iota(jnp.int32, (size, C), 1), bias[...], 0.0)
     shift = jnp.sum(column, axis=1, keepdims=True)
 
     @pl.loop(0, steps)
     def _(s):
-        f = jnp.concatenate([tile_of(feat, STEP * s + h) for h in range(STEP)], axis=1)
-        mix = dot(kron[...], f)
-        for h in range(STEP):
-            put_tile(field, STEP * s + h, mix[:, h * NZ : (h + 1) * NZ] + shift)
+        mix = dot(kron[...], batch_of(feat, s)) + shift
+        for h in range(BATCH):
+            at = pl.multiple_of((BATCH * s + h) * TILE, TILE)
+            for w, v in enumerate(unbatch(mix, h)):
+                field[:, pl.ds(at + w * EIGHT, EIGHT), :] = v
 
     @pl.loop(0, KZ // RING)
     def _(i):
@@ -561,36 +614,43 @@
         lhs = (dst_2[g].reshape(lines, GLANES) * lane_weight()).astype(BF)
         unfold(lhs, gz, ub)
 
-        @pl.loop(0, OCT // 2)
-        def _(p):
-            uv = ub[:, pl.ds(pl.multiple_of(p * PAIR, PAIR), PAIR)]
-            for r in range(0, cells, CHUNK):
-                res = dot(gy[r : r + CHUNK, :], uv)
+        parts = []
+        for p in range(OCT // 2):
+            uv = ub[:, p * PAIR : (p + 1) * PAIR]
+            outs = []
+            for d in range(duos):
+                res = dot(gy[d * DUO : (d + 1) * DUO, :], uv)
+                new = []
                 for h in range(2):
                     c = g * OCT + 2 * p + h
-                    for t in range(0, CHUNK, SUB):
-                        at = slice(r + t, r + t + SUB)
+                    pieces = []
+                    for t in range(0, DUO, SUB):
+                        at = slice(d * DUO + t, d * DUO + t + SUB)
                         x = res[t : t + SUB, h * NZ : (h + 1) * NZ] + field[c, at]
-                        pg[c, at] = (cot[c, at].astype(F32) * slope(x)).astype(BF)
-
-        out = forward_group(pg, g, fy, fz, lines) * lane_weight()
-        src_a[g] = out.reshape(n, rows, GLANES)
+                        v = (cot[c, at].astype(F32) * slope(x)).astype(BF)
+                        pg[c, at] = v
+                        pieces.append(v)
+                    new.append(jnp.concatenate(pieces, axis=0))
+                outs.append(dot(fy[...], jnp.concatenate(new, axis=1)).astype(BF))
+            parts += fold_pair(outs)
+        put_plane(parts, fz, lane_weight(), tmp, src_a, g, rows)
         send_group(n, 2, g, src_a, dst_3, send, recv)
 
     acc[...] = jnp.zeros_like(acc)
 
     @pl.loop(0, steps)
     def _(s):
-        f = jnp.concatenate([tile_of(feat, STEP * s + h) for h in range(STEP)], axis=1)
-        g = jnp.concatenate([tile_of(pg, STEP * s + h) for h in range(STEP)], axis=1)
-        acc[...] += lax.dot_general(g, f, (((1,), (1,)), ((), ())), preferred_element_type=F32)
+        acc[...] += lax.dot_general(
+            batch_of(pg, s), batch_of(feat, s), (((1,), (1,)), ((), ())),
+            preferred_element_type=F32,
+        )
 
     ri = lax.broadcasted_iota(jnp.int32, (size, size), 0)
     ci = lax.broadcasted_iota(jnp.int32, (size, size), 1)
-    masked = jnp.where(ri % TILE == ci % TILE, acc[...], 0.0)
-    rows_sum = jnp.sum(masked.reshape(C, TILE, size), axis=1)
+    masked = jnp.where(ri % EIGHT == ci % EIGHT, acc[...], 0.0)
+    rows_sum = jnp.sum(masked.reshape(C, EIGHT, size), axis=1)
     fold = jnp.where(
-        lax.broadcasted_iota(jnp.int32, (size, LANES), 0) // TILE
+        lax.broadcasted_iota(jnp.int32, (size, LANES), 0) // EIGHT
         == lax.broadcasted_iota(jnp.int32, (size, LANES), 1),
         1.0,
         0.0,
@@ -643,10 +703,10 @@
 
     @pl.loop(0, steps)
     def _(s):
-        f = jnp.concatenate([tile_of(pg, STEP * s + h) for h in range(STEP)], axis=1)
-        mix = dot(kron[...], f)
-        for h in range(STEP):
-            put_tile(cot, STEP * s + h, mix[:, h * NZ : (h + 1) * NZ].astype(BF))
+        mix = dot(kron[...], batch_of(pg, s))
+        for h in range(BATCH):
+            both = jnp.concatenate(unbatch(mix, h), axis=1).astype(BF)
+            put_tile(cot, BATCH * s + h, both.reshape(C * TILE, NZ))
 
     save = pltpu.make_async_copy(cot, mix_hbm, osem)
     save.start()
@@ -679,12 +739,8 @@
     vs = [v[g] for g in range(GROUPS)]
     ds = [d[g] for g in range(GROUPS)]
     for k in range(KZ):
-        full = diagonal(fill_lanes(gather_channels(vs, k)))
-        right = gather_channels(ds, k)[:, :C]
-        high, top = full.astype(BF), right.astype(BF)
-        rest, low_part = (full - high.astype(F32)).astype(BF), (right - top.astype(F32)).astype(BF)
-        left = jnp.concatenate([high, rest, high], axis=0)
-        side = jnp.concatenate([top, top, low_part], axis=0)
+        left = diagonal(fill_lanes(gather_channels(vs, k))).astype(BF)
+        side = gather_channels(ds, k)[:, :C].astype(BF)
         sg[k] = lax.dot_general(left, side, (((0,), (0,)), ((), ())), preferred_element_type=F32)
         pltpu.make_async_copy(sg.at[k], sg_hbm.at[k], ssem.at[k]).start()
     for copy in tables_in:
@@ -693,14 +749,13 @@
         loads[g].wait()
         unfold(back[g], gz, ub)
 
-        @pl.loop(0, OCT // 2)
-        def _(p):
-            uv = ub[:, pl.ds(pl.multiple_of(p * PAIR, PAIR), PAIR)]
-            for r in range(0, cells, CHUNK):
-                res = dot(gy[r : r + CHUNK, :], uv)
+        for p in range(OCT // 2):
+            uv = ub[:, p * PAIR : (p + 1) * PAIR]
+            for r in range(0, cells, DUO):
+                res = dot(gy[r : r + DUO, :], uv)
                 for h in range(2):
                     c = g * OCT + 2 * p + h
-                    at = slice(r, r + CHUNK)
+                    at = slice(r, r + DUO)
                     out[c, at] = (res[:, h * NZ : (h + 1) * NZ] + mix[c, at].astype(F32)).astype(BF)
 
         part = pl.ds(g * OCT, OCT)
@@ -714,13 +769,13 @@
 
 def fused_shards(n, rows, features, cotangent, spectral_weight, pointwise_weight, biases):
     known = tables(rows)
-    fy, gy, fx2, gx2, fz, gz = [jnp.asarray(known[i]) for i in (0, 1, 8, 9, 10, 11)]
+    gy, fx2, gx2, fz, gz, fy = [jnp.asarray(known[i]) for i in (1, 8, 9, 10, 11, 12)]
     cells = rows * NY
     lines = KY * rows
     dma = pltpu.SemaphoreType.DMA
     block = pltpu.VMEM((C, cells, NZ), BF)
     shape = jax.ShapeDtypeStruct
-    wide = C * TILE
+    wide = C * EIGHT
     swap = pltpu.VMEM((GROUPS, n, rows, GLANES), F32)
     spec = shape((GROUPS, 2 * KX, LANES), F32)
     mix, back, v, d, total = pl.pallas_call(
@@ -740,6 +795,7 @@
             pltpu.VMEM((2 * lines, OCT * NZ), BF), pltpu.VMEM((KZ, 2 * KX, LANES), F32),
             swap, swap, swap, swap, swap, swap,
             pltpu.VMEM((16, LANES), F32), pltpu.VMEM((n, 16, LANES), F32),
+            pltpu.VMEM((2, lines, LANES), F32),
             dma((GROUPS,)), dma((GROUPS,)), dma((4,)), dma((RING,)),
             dma((4, GROUPS)), dma((4, GROUPS)), dma, dma, dma,
         ],

time: 96.4 us -> 93.2 us (0.967)
  Pallas kernels: 95.6 us -> 92.2 us
    pallas_call x1, Pallas kernels: 78.4 us -> 76.4 us  [fused_shards(): pl.pallas_call(functools.partial(heart_kernel, rows, n), out_shape=[shape...]
    pallas_call x1, Pallas kernels: 17.2 us -> 15.8 us  [fused_shards(): pl.pallas_call(functools.partial(tail_kernel, rows), out_shape=[shape((C,...]
where the time goes in v2:
time: 93.2 us; the launch traced here: 93 us
  Pallas kernels  92.2 us (99%)
    pallas_call x1, Pallas kernels, fused_shards(): pl.pallas_call(functools.partial(heart_kernel, rows, n), out_shape=[shape...  76.4 us
    pallas_call x1, Pallas kernels, fused_shards(): pl.pallas_call(functools.partial(tail_kernel, rows), out_shape=[shape((C,...  15.8 us

profile of v2, /device:TPU:0, one launch (start us, length us, event | category | flops | bytes accessed | tf_op | source)
XLA Modules:
  0.0 93.0 jit_solution(5405690334240281167)
XLA Ops:
  0.6 76.4 %heart.1 = (bf16[32,1024,128]{2,1,0:T(8,128)(2,1)}, bf16[4,128,256]{2,1,0:T(8,128)(2,1)}, f32[4,32,128]{2,1,0:T(8,128)}, f32[4,32,128]{2,1,0:T(8,128)}, f32[16,128]{1,0:T(8,128)}) custom-call(bf16[32,1024,128]{2,1,0:T(8,128)(2,1)} %bitcast.7, bf16[32,1024,128]{2,1,0:T(8,128)(2,1)} %bitcast.8, f32[16,1024,32]{2,1,0:T(8,128)} %bitcast.9, ...), custom_call_target="tpu_custom_call" | custom-call | tf_op jit(solution)/shard_map/heart/pallas_call | solution.py:781
  77.0 15.8 %tail.1 = (bf16[32,1024,128]{2,1,0:T(8,128)(2,1)}, f32[16,1024,32]{2,1,0:T(8,128)}, f32[32,32]{1,0:T(8,128)}, f32[1,32]{1,0:T(1,128)}) custom-call(bf16[32,1024,128]{2,1,0:T(8,128)(2,1)} %get-tuple-element.13.mix_hbm, bf16[256,2048]{1,0:T(8,128)(2,1)} %constant.16.clone.gz_hbm, bf16[1024,256]{1,0:T(8,128)(2,1)} %constant.12.clone.gy_hbm, ...), custom_call_target="tpu_custom_call" | custom-call | tf_op jit(solution)/shard_map/tail/pallas_call | solution.py:811

commit v3 on v2

--- a/solution.py
+++ b/solution.py
@@ -352,6 +352,7 @@
 FULL = 2 * KX * C
 ONE = 1.0 / SCALE
 RING = 8
+QUAD = 4
 EIGHT = 8
 BATCH = 16
 PAIR = 2 * NZ
@@ -369,28 +370,82 @@
     return jnp.where(k == 0, SCALE, 2.0 * SCALE)
 
 
-def send_group(n, turn, g, src, dst, send, recv):
+def place():
     me = lax.axis_index("mp")
-
-    @pl.loop(1, n)
-    def _(s):
-        peer = lax.rem(me + s, n)
-        remote(src.at[g, peer], dst.at[g, me], send.at[turn, g], recv.at[turn, g], peer).start()
-
-    pltpu.make_async_copy(src.at[g, me], dst.at[g, me], recv.at[turn, g]).start()
+    return me // QUAD, lax.rem(me, QUAD)
+
+
+def near_peers():
+    slab, spot = place()
+    mates = [lax.rem(spot + s, QUAD) for s in range(1, QUAD)]
+    return [(mate, slab * QUAD + mate) for mate in mates]
+
+
+def far_peers(slabs):
+    slab, spot = place()
+    others = [lax.rem(slab + s, slabs) for s in range(1, slabs)]
+    return [(other, other * QUAD + spot) for other in others]
+
+
+def meet(slabs):
+    barrier = pltpu.get_barrier_semaphore()
+    for _, peer in near_peers() + far_peers(slabs):
+        pl.semaphore_signal(
+            barrier, inc=1, device_id={"mp": peer}, device_id_type=pl.DeviceIdType.MESH
+        )
+
+
+def send_near(turn, g, src, dst, send, recv):
+    _, spot = place()
+    for mate, peer in near_peers():
+        remote(src.at[g, mate], dst.at[g, spot], send.at[turn, g], recv.at[turn, g], peer).start()
+    pltpu.make_async_copy(src.at[g, spot], dst.at[g, spot], recv.at[turn, g]).start()
+
+
+def send_far(turn, g, pick, dst, send, recv, slabs):
+    slab, _ = place()
+    for other, peer in far_peers(slabs):
+        remote(pick(other), dst.at[g, slab], send.at[turn, g], recv.at[turn, g], peer).start()
+    pltpu.make_async_copy(pick(slab), dst.at[g, slab], recv.at[turn, g]).start()
 
 
 def wait_bytes(ref, sem):
     pltpu.make_async_copy(ref, ref, sem).wait()
 
 
-def wait_sent(n, turn, g, src, send):
-    wait_bytes(src.at[g, pl.ds(0, n - 1)], send.at[turn, g])
-
-
-def spectrum(dst, g, fx2):
-    pair = [dst[g, :, :, r * HALF : (r + 1) * HALF].reshape(NX, HALF) for r in range(2)]
-    return sharp(fx2[...], jnp.concatenate(pair, axis=0))
+def wait_sent(turn, g, like, send):
+    wait_bytes(like.at[g, pl.ds(0, like.shape[1] - 1)], send.at[turn, g])
+
+
+def part_lines(near, g, fxs, far):
+    slab, _ = place()
+    columns = []
+    for t in range(near.shape[2]):
+        pair = [
+            near[g, :, t, :, r * HALF : (r + 1) * HALF].reshape(fxs.shape[2] // 2, HALF)
+            for r in range(2)
+        ]
+        columns.append(jnp.concatenate(pair, axis=0))
+    res = sharp(fxs[slab], jnp.concatenate(columns, axis=1))
+    for t in range(near.shape[2]):
+        far[g, t] = res[:, t * HALF : (t + 1) * HALF]
+
+
+def sum_lines(far, g):
+    return sum(far[g, t] for t in range(1, far.shape[1])) + far[g, 0]
+
+
+def spread_lines(far, g, gxs, src):
+    slab, _ = place()
+    rows = src.shape[3]
+    both = sharp(gxs[slab], jnp.concatenate([far[g, z] for z in range(far.shape[1])], axis=1))
+    for r in range(2):
+        for q in range(QUAD):
+            top = (r * QUAD + q) * rows
+            for z in range(far.shape[1]):
+                src[g, q, z, :, r * HALF : (r + 1) * HALF] = both[
+                    top : top + rows, z * HALF : (z + 1) * HALF
+                ]
 
 
 def gather_channels(parts, k):
@@ -426,15 +481,6 @@
         shift = (k * OCT - g * OCT) % LANES
         moved = pltpu.roll(v, shift, 1) if shift else v
         parts[g] = jnp.where(lane == k, moved, parts[g])
-
-
-def lines_out(parts, gx2, src, n):
-    for g in range(GROUPS):
-        both = sharp(gx2[...], parts[g])
-        for r in range(2):
-            src[g, :, :, r * HALF : (r + 1) * HALF] = both[r * NX : (r + 1) * NX].reshape(
-                n, NX // n, HALF
-            )
 
 
 def halves(ref, t):
@@ -492,7 +538,9 @@
         tmp[r] = res[:, r * HALF : (r + 1) * HALF]
     for j in range(KY):
         for r in range(2):
-            src[g, j, :, r * HALF : (r + 1) * HALF] = tmp[r, pl.ds(j, rows, stride=KY), :]
+            src[g, j % QUAD, j // QUAD, :, r * HALF : (r + 1) * HALF] = tmp[
+                r, pl.ds(j, rows, stride=KY), :
+            ]
 
 
 def unfold(lhs, gz, ub):
@@ -505,17 +553,20 @@
 
 
 def heart_kernel(
-    rows, n, feat_hbm, cot_hbm, w_hbm, fy_hbm, fz_hbm, gy_hbm, gz_hbm, weight, bias, fx2, gx2,
+    rows, n, feat_hbm, cot_hbm, w_hbm, fy_hbm, fz_hbm, gy_hbm, gz_hbm, weight, bias, fxs, gxs,
     mix_hbm, back, vout, dout, total,
     feat, cot, pg, field, ring, wb, fy, fz, gy, gz, kron, acc, ub, stage, src_a, src_b,
-    dst_1, dst_2, dst_3, dst_4, sums, every, tmp, fsem, csem, tsem, wsem, send, recv, ssem, rsem, osem,
+    near_1, near_2, near_3, near_4, out_f, out_m, far_1, far_2, far_3, far_4,
+    sums, sums_near, sums_mid, sums_far, tmp, fsem, csem, tsem, wsem, send, recv, ssem, rsem, osem,
 ):
     me = lax.axis_index("mp")
     cells = rows * NY
     lines = KY * rows
     steps = cells // (BATCH * TILE)
     duos = cells // DUO
-    greet(n)
+    slabs = n // QUAD
+    slab, spot = place()
+    meet(slabs)
     early = [pltpu.make_async_copy(a, b, tsem.at[i]) for i, (a, b) in enumerate(((fy_hbm, fy), (fz_hbm, fz)))]
     late = [pltpu.make_async_copy(a, b, tsem.at[2 + i]) for i, (a, b) in enumerate(((gy_hbm, gy), (gz_hbm, gz)))]
 
@@ -553,9 +604,22 @@
 
         @pl.when(g == 0)
         def _():
-            pl.semaphore_wait(pltpu.get_barrier_semaphore(), n - 1)
-
-        send_group(n, 0, g, src_a, dst_1, send, recv)
+            pl.semaphore_wait(pltpu.get_barrier_semaphore(), QUAD + slabs - 2)
+
+        send_near(0, g, src_a, near_1, send, recv)
+
+    def reduce_group(turn, g, near, far):
+        wait_bytes(near.at[g], recv.at[turn, g])
+        part_lines(near, g, fxs, out_f)
+        send_far(turn + 1, g, lambda t: out_f.at[g, t], far, send, recv, slabs)
+
+    def give_group(turn, g, far):
+        send_far(turn, g, lambda t: out_m.at[g], far, send, recv, slabs)
+
+    def open_group(turn, g, far, near):
+        wait_bytes(far.at[g], recv.at[turn, g])
+        spread_lines(far, g, gxs, src_b)
+        send_near(turn + 1, g, src_b, near, send, recv)
 
     for k in range(RING):
         ring_copy(k, k).start()
@@ -577,6 +641,7 @@
             at = pl.multiple_of((BATCH * s + h) * TILE, TILE)
             for w, v in enumerate(unbatch(mix, h)):
                 field[:, pl.ds(at + w * EIGHT, EIGHT), :] = v
+        reduce_group(0, s, near_1, far_1)
 
     @pl.loop(0, KZ // RING)
     def _(i):
@@ -590,8 +655,8 @@
                 ring_copy(k + RING, slot).start()
 
     for g in range(GROUPS):
-        wait_bytes(dst_1.at[g], recv.at[0, g])
-        vout[g] = spectrum(dst_1, g, fx2)
+        wait_bytes(far_1.at[g], recv.at[1, g])
+        vout[g] = sum_lines(far_1, g)
     parts = [vout[g] for g in range(GROUPS)]
     mixed = [jnp.zeros((2 * KX, LANES), F32) for _ in range(GROUPS)]
     for k in range(KZ):
@@ -599,19 +664,25 @@
         stage[k, :, :C] = dot(left, wb[k])
     for k in range(KZ):
         put_channels(mixed, k, stage[k])
-    lines_out(mixed, gx2, src_b, n)
-    for g in range(GROUPS):
-        send_group(n, 1, g, src_b, dst_2, send, recv)
+    for g in range(GROUPS):
+        out_m[g] = mixed[g]
+        give_group(2, g, far_2)
     for copy in late:
         copy.wait()
     for g in range(GROUPS):
-        wait_sent(n, 0, g, src_a, send)
+        wait_sent(0, g, src_a, send)
+        wait_sent(1, g, out_f, send)
         cot_copy(g).wait()
+    open_group(2, 0, far_2, near_2)
 
     @pl.loop(0, GROUPS)
     def _(g):
-        wait_bytes(dst_2.at[g], recv.at[1, g])
-        lhs = (dst_2[g].reshape(lines, GLANES) * lane_weight()).astype(BF)
+        @pl.when(g + 1 < GROUPS)
+        def _():
+            open_group(2, g + 1, far_2, near_2)
+
+        wait_bytes(near_2.at[g], recv.at[3, g])
+        lhs = (near_2[g].reshape(lines, GLANES) * lane_weight()).astype(BF)
         unfold(lhs, gz, ub)
 
         parts = []
@@ -634,7 +705,11 @@
                 outs.append(dot(fy[...], jnp.concatenate(new, axis=1)).astype(BF))
             parts += fold_pair(outs)
         put_plane(parts, fz, lane_weight(), tmp, src_a, g, rows)
-        send_group(n, 2, g, src_a, dst_3, send, recv)
+        send_near(4, g, src_a, near_3, send, recv)
+
+        @pl.when(g > 0)
+        def _():
+            reduce_group(4, g - 1, near_3, far_3)
 
     acc[...] = jnp.zeros_like(acc)
 
@@ -644,6 +719,10 @@
             batch_of(pg, s), batch_of(feat, s), (((1,), (1,)), ((), ())),
             preferred_element_type=F32,
         )
+
+        @pl.when(s == steps - 2)
+        def _():
+            reduce_group(4, GROUPS - 1, near_3, far_3)
 
     ri = lax.broadcasted_iota(jnp.int32, (size, size), 0)
     ci = lax.broadcasted_iota(jnp.int32, (size, size), 1)
@@ -663,8 +742,8 @@
     kron[...] = widen_with(weight[...], True)
 
     for g in range(GROUPS):
-        wait_bytes(dst_3.at[g], recv.at[2, g])
-        dout[g] = spectrum(dst_3, g, fx2)
+        wait_bytes(far_3.at[g], recv.at[5, g])
+        dout[g] = sum_lines(far_3, g)
     parts = [dout[g] for g in range(GROUPS)]
     dc = jnp.zeros((1, LANES), F32)
     lane = lax.broadcasted_iota(jnp.int32, (1, LANES), 1)
@@ -689,17 +768,14 @@
         both = a0 + jnp.concatenate([a1[KX:], -a1[:KX]], axis=0)
         put_channels(mixed, k, fill_lanes(both))
     for g in range(GROUPS):
-        wait_sent(n, 1, g, src_b, send)
-    lines_out(mixed, gx2, src_b, n)
-    for g in range(GROUPS):
-        send_group(n, 3, g, src_b, dst_4, send, recv)
-
-    @pl.loop(1, n)
-    def _(s):
-        peer = lax.rem(me + s, n)
-        remote(sums, every.at[me], ssem, rsem, peer).start()
-
-    pltpu.make_async_copy(sums, every.at[me], rsem).start()
+        wait_sent(2, g, far_2, send)
+        wait_sent(3, g, src_b, send)
+    for g in range(GROUPS):
+        out_m[g] = mixed[g]
+        give_group(6, g, far_4)
+    for _, peer in near_peers():
+        remote(sums, sums_near.at[spot], ssem.at[0], rsem.at[0], peer).start()
+    pltpu.make_async_copy(sums, sums_near.at[spot], rsem.at[0]).start()
 
     @pl.loop(0, steps)
     def _(s):
@@ -707,18 +783,27 @@
         for h in range(BATCH):
             both = jnp.concatenate(unbatch(mix, h), axis=1).astype(BF)
             put_tile(cot, BATCH * s + h, both.reshape(C * TILE, NZ))
+        open_group(6, s, far_4, near_4)
 
     save = pltpu.make_async_copy(cot, mix_hbm, osem)
     save.start()
-    for g in range(GROUPS):
-        wait_bytes(dst_4.at[g], recv.at[3, g])
-        back[g] = dst_4[g].reshape(lines, GLANES).astype(BF)
-    wait_bytes(every, rsem)
-    total[...] = jnp.sum(every[...], axis=0) * float(NX * NY * NZ) ** (-0.5)
-    wait_bytes(every.at[pl.ds(0, n - 1)], ssem)
-    for g in range(GROUPS):
-        wait_sent(n, 2, g, src_a, send)
-        wait_sent(n, 3, g, src_b, send)
+    wait_bytes(sums_near, rsem.at[0])
+    sums_mid[...] = jnp.sum(sums_near[...], axis=0)
+    for _, peer in far_peers(slabs):
+        remote(sums_mid, sums_far.at[slab], ssem.at[1], rsem.at[1], peer).start()
+    pltpu.make_async_copy(sums_mid, sums_far.at[slab], rsem.at[1]).start()
+    for g in range(GROUPS):
+        wait_bytes(near_4.at[g], recv.at[7, g])
+        back[g] = near_4[g].reshape(lines, GLANES).astype(BF)
+    wait_bytes(sums_far, rsem.at[1])
+    total[...] = jnp.sum(sums_far[...], axis=0) * float(NX * NY * NZ) ** (-0.5)
+    wait_bytes(sums_near.at[pl.ds(0, QUAD - 1)], ssem.at[0])
+    wait_bytes(sums_far.at[pl.ds(0, slabs - 1)], ssem.at[1])
+    for g in range(GROUPS):
+        wait_sent(4, g, src_a, send)
+        wait_sent(5, g, out_f, send)
+        wait_sent(6, g, far_4, send)
+        wait_sent(7, g, src_b, send)
     save.wait()
 
 
@@ -769,14 +854,24 @@
 
 def fused_shards(n, rows, features, cotangent, spectral_weight, pointwise_weight, biases):
     known = tables(rows)
-    gy, fx2, gx2, fz, gz, fy = [jnp.asarray(known[i]) for i in (1, 8, 9, 10, 11, 12)]
+    fz, gz, fy = [jnp.asarray(known[i]) for i in (10, 11, 12)]
     cells = rows * NY
     lines = KY * rows
+    slabs = n // QUAD
+    tall = QUAD * rows
+    gy = known[1].reshape(cells, 2, slabs, QUAD, rows).transpose(0, 1, 3, 2, 4)
+    gy = jnp.asarray(gy.reshape(known[1].shape))
+    fxs = known[8].reshape(2 * KX, 2, slabs, tall).transpose(2, 0, 1, 3)
+    fxs = jnp.asarray(fxs.reshape(slabs, 2 * KX, 2 * tall))
+    gxs = known[9].reshape(2, slabs, tall, 2 * KX).transpose(1, 0, 2, 3)
+    gxs = jnp.asarray(gxs.reshape(slabs, 2 * tall, 2 * KX))
     dma = pltpu.SemaphoreType.DMA
     block = pltpu.VMEM((C, cells, NZ), BF)
     shape = jax.ShapeDtypeStruct
     wide = C * EIGHT
-    swap = pltpu.VMEM((GROUPS, n, rows, GLANES), F32)
+    swap = pltpu.VMEM((GROUPS, QUAD, slabs, rows, GLANES), F32)
+    far = pltpu.VMEM((GROUPS, slabs, 2 * KX, LANES), F32)
+    few = pltpu.VMEM((16, LANES), F32)
     spec = shape((GROUPS, 2 * KX, LANES), F32)
     mix, back, v, d, total = pl.pallas_call(
         functools.partial(heart_kernel, rows, n),
@@ -793,11 +888,12 @@
             pltpu.VMEM(gy.shape, BF), pltpu.VMEM(gz.shape, BF),
             pltpu.VMEM((wide, wide), BF), pltpu.VMEM((wide, wide), F32),
             pltpu.VMEM((2 * lines, OCT * NZ), BF), pltpu.VMEM((KZ, 2 * KX, LANES), F32),
-            swap, swap, swap, swap, swap, swap,
-            pltpu.VMEM((16, LANES), F32), pltpu.VMEM((n, 16, LANES), F32),
+            swap, swap, swap, swap, swap, swap, far,
+            pltpu.VMEM((GROUPS, 2 * KX, LANES), F32), far, far, far, far,
+            few, pltpu.VMEM((QUAD, 16, LANES), F32), few, pltpu.VMEM((slabs, 16, LANES), F32),
             pltpu.VMEM((2, lines, LANES), F32),
             dma((GROUPS,)), dma((GROUPS,)), dma((4,)), dma((RING,)),
-            dma((4, GROUPS)), dma((4, GROUPS)), dma, dma, dma,
+            dma((8, GROUPS)), dma((8, GROUPS)), dma((2,)), dma((2,)), dma,
         ],
         compiler_params=pltpu.CompilerParams(
             collective_id=1, has_side_effects=True, vmem_limit_bytes=62 << 20
@@ -806,7 +902,7 @@
     )(
         features.reshape(C, cells, NZ), cotangent.reshape(C, cells, NZ),
         spectral_weight.reshape(KZ, FULL, C), fy, fz, gy, gz, pointwise_weight,
-        biases.reshape(1, C), fx2, gx2,
+        biases.reshape(1, C), fxs, gxs,
     )
     grad, sg, pwg, bg = pl.pallas_call(
         functools.partial(tail_kernel, rows),

time: 93.2 us -> 91 us (0.976)
  Pallas kernels: 92.2 us -> 90 us
    pallas_call x1, Pallas kernels: 76.4 us -> 74.2 us  [fused_shards(): pl.pallas_call(functools.partial(heart_kernel, rows, n), out_shape=[shape...]
where the time goes in v3:
time: 91 us; the launch traced here: 90.8 us
  Pallas kernels  90 us (99%)
    pallas_call x1, Pallas kernels, fused_shards(): pl.pallas_call(functools.partial(heart_kernel, rows, n), out_shape=[shape...  74.2 us
    pallas_call x1, Pallas kernels, fused_shards(): pl.pallas_call(functools.partial(tail_kernel, rows), out_shape=[shape((C,...  15.8 us

profile of v3, /device:TPU:0, one launch (start us, length us, event | category | flops | bytes accessed | tf_op | source)
XLA Modules:
  0.0 90.8 jit_solution(6715390139536226122)
XLA Ops:
  0.6 74.2 %heart.1 = (bf16[32,1024,128]{2,1,0:T(8,128)(2,1)}, bf16[4,128,256]{2,1,0:T(8,128)(2,1)}, f32[4,32,128]{2,1,0:T(8,128)}, f32[4,32,128]{2,1,0:T(8,128)}, f32[16,128]{1,0:T(8,128)}) custom-call(bf16[32,1024,128]{2,1,0:T(8,128)(2,1)} %bitcast.7, bf16[32,1024,128]{2,1,0:T(8,128)(2,1)} %bitcast.8, f32[16,1024,32]{2,1,0:T(8,128)} %bitcast.9, ...), custom_call_target="tpu_custom_call" | custom-call | tf_op jit(solution)/shard_map/heart/pallas_call | solution.py:876
  74.8 15.8 %tail.1 = (bf16[32,1024,128]{2,1,0:T(8,128)(2,1)}, f32[16,1024,32]{2,1,0:T(8,128)}, f32[32,32]{1,0:T(8,128)}, f32[1,32]{1,0:T(1,128)}) custom-call(bf16[32,1024,128]{2,1,0:T(8,128)(2,1)} %get-tuple-element.13.mix_hbm, bf16[256,2048]{1,0:T(8,128)(2,1)} %constant.13.clone.gz_hbm, bf16[1024,256]{1,0:T(8,128)(2,1)} %constant.15.clone.gy_hbm, ...), custom_call_target="tpu_custom_call" | custom-call | tf_op jit(solution)/shard_map/tail/pallas_call | solution.py:907

commit v4 on v3

--- a/solution.py
+++ b/solution.py
@@ -815,7 +815,14 @@
     tables_in = [pltpu.make_async_copy(a, b, tsem.at[i]) for i, (a, b) in enumerate(((gz_hbm, gz), (gy_hbm, gy)))]
     for copy in tables_in:
         copy.start()
-    loads = load_groups(mix_hbm, mix, msem)
+    loads = [
+        pltpu.make_async_copy(
+            mix_hbm.at[pl.ds(g * OCT, OCT)], mix.at[pl.ds(g * OCT, OCT)], msem.at[g]
+        )
+        for g in range(GROUPS)
+    ]
+    for copy in loads[:2]:
+        copy.start()
     t = total[...]
     for i in range(C // 8):
         part = pltpu.roll(t[:8], LANES - i * C, 1) if i else t[:8]
@@ -823,15 +830,21 @@
     bg[...] = t[8:9, :C]
     vs = [v[g] for g in range(GROUPS)]
     ds = [d[g] for g in range(GROUPS)]
-    for k in range(KZ):
-        left = diagonal(fill_lanes(gather_channels(vs, k))).astype(BF)
-        side = gather_channels(ds, k)[:, :C].astype(BF)
-        sg[k] = lax.dot_general(left, side, (((0,), (0,)), ((), ())), preferred_element_type=F32)
-        pltpu.make_async_copy(sg.at[k], sg_hbm.at[k], ssem.at[k]).start()
-    for copy in tables_in:
-        copy.wait()
-    for g in range(GROUPS):
+    each = KZ // GROUPS
+    for g in range(GROUPS):
+        for k in range(g * each, (g + 1) * each):
+            left = diagonal(fill_lanes(gather_channels(vs, k))).astype(BF)
+            side = gather_channels(ds, k)[:, :C].astype(BF)
+            sg[k] = lax.dot_general(
+                left, side, (((0,), (0,)), ((), ())), preferred_element_type=F32
+            )
+            pltpu.make_async_copy(sg.at[k], sg_hbm.at[k], ssem.at[k]).start()
+        if g == 0:
+            for copy in tables_in:
+                copy.wait()
         loads[g].wait()
+        if g + 2 < GROUPS:
+            loads[g + 2].start()
         unfold(back[g], gz, ub)
 
         for p in range(OCT // 2):

time: 91 us -> 86.7 us (0.953)
  Pallas kernels: 90 us -> 85.7 us
    pallas_call x1, Pallas kernels: 15.8 us -> 11.5 us  [fused_shards(): pl.pallas_call(functools.partial(tail_kernel, rows), out_shape=[shape((C,...]
where the time goes in v4:
time: 86.7 us; the launch traced here: 86.5 us
  Pallas kernels  85.7 us (99%)
    pallas_call x1, Pallas kernels, fused_shards(): pl.pallas_call(functools.partial(heart_kernel, rows, n), out_shape=[shape...  74.2 us
    pallas_call x1, Pallas kernels, fused_shards(): pl.pallas_call(functools.partial(tail_kernel, rows), out_shape=[shape((C,...  11.5 us

profile of v4, /device:TPU:0, one launch (start us, length us, event | category | flops | bytes accessed | tf_op | source)
XLA Modules:
  0.0 86.5 jit_solution(6891705156717737367)
XLA Ops:
  0.6 74.2 %heart.1 = (bf16[32,1024,128]{2,1,0:T(8,128)(2,1)}, bf16[4,128,256]{2,1,0:T(8,128)(2,1)}, f32[4,32,128]{2,1,0:T(8,128)}, f32[4,32,128]{2,1,0:T(8,128)}, f32[16,128]{1,0:T(8,128)}) custom-call(bf16[32,1024,128]{2,1,0:T(8,128)(2,1)} %bitcast.7, bf16[32,1024,128]{2,1,0:T(8,128)(2,1)} %bitcast.8, f32[16,1024,32]{2,1,0:T(8,128)} %bitcast.9, ...), custom_call_target="tpu_custom_call" | custom-call | tf_op jit(solution)/shard_map/heart/pallas_call | solution.py:889
  74.8 11.5 %tail.1 = (bf16[32,1024,128]{2,1,0:T(8,128)(2,1)}, f32[16,1024,32]{2,1,0:T(8,128)}, f32[32,32]{1,0:T(8,128)}, f32[1,32]{1,0:T(1,128)}) custom-call(bf16[32,1024,128]{2,1,0:T(8,128)(2,1)} %get-tuple-element.13.mix_hbm, bf16[256,2048]{1,0:T(8,128)(2,1)} %constant.13.clone.gz_hbm, bf16[1024,256]{1,0:T(8,128)(2,1)} %constant.15.clone.gy_hbm, ...), custom_call_target="tpu_custom_call" | custom-call | tf_op jit(solution)/shard_map/tail/pallas_call | solution.py:920

commit v5 on v4

--- a/solution.py
+++ b/solution.py
@@ -591,6 +591,12 @@
     @pl.loop(0, GROUPS)
     def _(g):
         feat_copy(g).wait()
+
+        @pl.when(g == GROUPS - 2)
+        def _():
+            for k in range(RING):
+                ring_copy(k, k).start()
+
         parts = []
         for q in range(0, OCT, 2):
             c = g * OCT + q
@@ -621,8 +627,6 @@
         spread_lines(far, g, gxs, src_b)
         send_near(turn + 1, g, src_b, near, send, recv)
 
-    for k in range(RING):
-        ring_copy(k, k).start()
     for copy in late:
         copy.start()
     for g in range(GROUPS):
@@ -633,6 +637,16 @@
     row = lax.broadcasted_iota(jnp.int32, (size, C), 0) // EIGHT
     column = jnp.where(row == lax.broadcasted_iota(jnp.int32, (size, C), 1), bias[...], 0.0)
     shift = jnp.sum(column, axis=1, keepdims=True)
+
+    def take_weights(i):
+        for slot in range(RING):
+            k = i * RING + slot
+            ring_copy(k, slot).wait()
+            wb[k] = ring[slot].astype(BF)
+            if k + RING < KZ:
+                ring_copy(k + RING, slot).start()
+
+    take_weights(0)
 
     @pl.loop(0, steps)
     def _(s):
@@ -643,17 +657,8 @@
                 field[:, pl.ds(at + w * EIGHT, EIGHT), :] = v
         reduce_group(0, s, near_1, far_1)
 
-    @pl.loop(0, KZ // RING)
-    def _(i):
-        for slot in range(RING):
-            k = i * RING + slot
-            ring_copy(k, slot).wait()
-            wb[k] = ring[slot].astype(BF)
-
-            @pl.when(k + RING < KZ)
-            def _():
-                ring_copy(k + RING, slot).start()
-
+    for i in range(1, KZ // RING):
+        take_weights(i)
     for g in range(GROUPS):
         wait_bytes(far_1.at[g], recv.at[1, g])
         vout[g] = sum_lines(far_1, g)
@@ -777,21 +782,27 @@
         remote(sums, sums_near.at[spot], ssem.at[0], rsem.at[0], peer).start()
     pltpu.make_async_copy(sums, sums_near.at[spot], rsem.at[0]).start()
 
+    def save_copy(s):
+        part = pl.ds(pl.multiple_of(s * BATCH * TILE, BATCH * TILE), BATCH * TILE)
+        return pltpu.make_async_copy(cot.at[:, part], mix_hbm.at[:, part], osem.at[s])
+
     @pl.loop(0, steps)
     def _(s):
         mix = dot(kron[...], batch_of(pg, s))
         for h in range(BATCH):
             both = jnp.concatenate(unbatch(mix, h), axis=1).astype(BF)
             put_tile(cot, BATCH * s + h, both.reshape(C * TILE, NZ))
+        save_copy(s).start()
         open_group(6, s, far_4, near_4)
 
-    save = pltpu.make_async_copy(cot, mix_hbm, osem)
-    save.start()
-    wait_bytes(sums_near, rsem.at[0])
-    sums_mid[...] = jnp.sum(sums_near[...], axis=0)
-    for _, peer in far_peers(slabs):
-        remote(sums_mid, sums_far.at[slab], ssem.at[1], rsem.at[1], peer).start()
-    pltpu.make_async_copy(sums_mid, sums_far.at[slab], rsem.at[1]).start()
+        @pl.when(s == 1)
+        def _():
+            wait_bytes(sums_near, rsem.at[0])
+            sums_mid[...] = jnp.sum(sums_near[...], axis=0)
+            for _, peer in far_peers(slabs):
+                remote(sums_mid, sums_far.at[slab], ssem.at[1], rsem.at[1], peer).start()
+            pltpu.make_async_copy(sums_mid, sums_far.at[slab], rsem.at[1]).start()
+
     for g in range(GROUPS):
         wait_bytes(near_4.at[g], recv.at[7, g])
         back[g] = near_4[g].reshape(lines, GLANES).astype(BF)
@@ -804,7 +815,8 @@
         wait_sent(5, g, out_f, send)
         wait_sent(6, g, far_4, send)
         wait_sent(7, g, src_b, send)
-    save.wait()
+    for s in range(steps):
+        save_copy(s).wait()
 
 
 def tail_kernel(
@@ -906,7 +918,8 @@
             few, pltpu.VMEM((QUAD, 16, LANES), F32), few, pltpu.VMEM((slabs, 16, LANES), F32),
             pltpu.VMEM((2, lines, LANES), F32),
             dma((GROUPS,)), dma((GROUPS,)), dma((4,)), dma((RING,)),
-            dma((8, GROUPS)), dma((8, GROUPS)), dma((2,)), dma((2,)), dma,
+            dma((8, GROUPS)), dma((8, GROUPS)), dma((2,)), dma((2,)),
+            dma((cells // (BATCH * TILE),)),
         ],
         compiler_params=pltpu.CompilerParams(
             collective_id=1, has_side_effects=True, vmem_limit_bytes=62 << 20

time: 86.7 us -> 86.3 us (level)
  no operation moved by 1% of the time
where the time goes in v5:
time: 86.3 us; the launch traced here: 86.1 us
  Pallas kernels  85.3 us (99%)
    pallas_call x1, Pallas kernels, fused_shards(): pl.pallas_call(functools.partial(heart_kernel, rows, n), out_shape=[shape...  73.8 us
    pallas_call x1, Pallas kernels, fused_shards(): pl.pallas_call(functools.partial(tail_kernel, rows), out_shape=[shape((C,...  11.5 us

profile of v5, /device:TPU:0, one launch (start us, length us, event | category | flops | bytes accessed | tf_op | source)
XLA Modules:
  0.0 86.1 jit_solution(13974865088553151495)
XLA Ops:
  0.6 73.8 %heart.1 = (bf16[32,1024,128]{2,1,0:T(8,128)(2,1)}, bf16[4,128,256]{2,1,0:T(8,128)(2,1)}, f32[4,32,128]{2,1,0:T(8,128)}, f32[4,32,128]{2,1,0:T(8,128)}, f32[16,128]{1,0:T(8,128)}) custom-call(bf16[32,1024,128]{2,1,0:T(8,128)(2,1)} %bitcast.7, bf16[32,1024,128]{2,1,0:T(8,128)(2,1)} %bitcast.8, f32[16,1024,32]{2,1,0:T(8,128)} %bitcast.9, ...), custom_call_target="tpu_custom_call" | custom-call | tf_op jit(solution)/shard_map/heart/pallas_call | solution.py:901
  74.4 11.5 %tail.1 = (bf16[32,1024,128]{2,1,0:T(8,128)(2,1)}, f32[16,1024,32]{2,1,0:T(8,128)}, f32[32,32]{1,0:T(8,128)}, f32[1,32]{1,0:T(1,128)}) custom-call(bf16[32,1024,128]{2,1,0:T(8,128)(2,1)} %get-tuple-element.13.mix_hbm, bf16[256,2048]{1,0:T(8,128)(2,1)} %constant.13.clone.gz_hbm, bf16[1024,256]{1,0:T(8,128)(2,1)} %constant.15.clone.gy_hbm, ...), custom_call_target="tpu_custom_call" | custom-call | tf_op jit(solution)/shard_map/tail/pallas_call | solution.py:933
